TPU v7x, 1024 devices: a whole 4x4x32 slice. The times are simulated.
1024 devices in a mesh: outer: 64 (over z_lo, x, core), inner: 16 (over y, z_hi).
Axes of the slice: x: 4, y: 4, z: 32 (z_hi: 4, z_lo: 8; z = z_hi * 8 + z_lo), core: 2. Of those that a mesh axis runs over, the one named last changes fastest.
Arguments:
- hidden: bfloat16 [245760, 7168], P(('outer', 'inner')), may hold values from -24 to 24
- segment_ids: int32 [1024, 240], P(('outer', 'inner')), may hold values from 0 to 59, never falling along the last dimension, each value on 1 to 120 neighbouring positions
- key_grad: bfloat16 [245760, 64], P(('outer', 'inner')), may hold values from -0.024169922 to 0.024169922
- weight_bf16: bfloat16 [7168, 64], replicated, may hold values from -0.75 to 0.75
- gain_bf16: bfloat16 [7168], replicated, may hold values from 0.099609375 to 1.8984375
- weight_master: float32 [7168, 64], P(('outer', 'inner')), may hold values from -0.018 to 0.018
- weight_first: float32 [7168, 64], P(('outer', 'inner')), may hold values from -6 to 6
- weight_second: float32 [7168, 64], P(('outer', 'inner')), may hold values from 0.1 to 10
- gain_master: float32 [7168], P(('outer', 'inner')), may hold values from 0.1 to 1.9
- gain_first: float32 [7168], P(('outer', 'inner')), may hold values from -6 to 6
- gain_second: float32 [7168], P(('outer', 'inner')), may hold values from 0.1 to 10
Outputs:
- weight_master_new: float32 [7168, 64], P(('outer', 'inner'))
- weight_first_new: float32 [7168, 64], P(('outer', 'inner'))
- weight_second_new: float32 [7168, 64], P(('outer', 'inner'))
- gain_master_new: float32 [7168], P(('outer', 'inner'))
- gain_first_new: float32 [7168], P(('outer', 'inner'))
- gain_second_new: float32 [7168], P(('outer', 'inner'))
- weight_bf16_new: bfloat16 [7168, 64], replicated
- gain_bf16_new: bfloat16 [7168], replicated
Inputs may be any that keep to these rules, and one draw needn't show every extreme that they name: `segment_ids`: in each row the ids never fall; each segment spans 1 to 120 tokens, one exactly that many.
All inputs are finite; a program needn't handle non-finite values.
Results may differ from a plain program's by a relative error of at most 0.0055.
Values may be sent and summed in bfloat16 or wider, within the bound.
A program may use at most 32 MiB of HBM per device.

v0:
```python
import jax
import jax.numpy as jnp
from jax import lax
from jax.sharding import PartitionSpec as P

STEP = 20


beta_one = 0.9
beta_two = 0.95
learning_rate = 0.00022
adam_epsilon = 1e-08
norm_epsilon = 1e-06


def rotate_back(gradient, segment_row):
    length = segment_row.shape[0]
    places = jnp.arange(length, dtype=jnp.int32)
    same_segment = segment_row[:, None] == segment_row[None, :]
    starts = jnp.min(jnp.where(same_segment, places[None, :], length), axis=1)
    positions = (places - starts).astype(jnp.float32)
    half_width = gradient.shape[1] // 2
    frequency = 10000.0 ** (-jnp.arange(half_width, dtype=jnp.float32) / half_width)
    angles = positions[:, None] * frequency[None, :]
    cosine_table = jnp.cos(angles)
    sine_table = jnp.sin(angles)
    first_half = gradient[:, :half_width].astype(jnp.float32)
    second_half = gradient[:, half_width:].astype(jnp.float32)
    joined = jnp.concatenate(
        [
            first_half * cosine_table + second_half * sine_table,
            second_half * cosine_table - first_half * sine_table,
        ],
        axis=1,
    )
    return joined.astype(jnp.bfloat16)


def local_terms(hidden_rows, segment_row, grad_rows, weight_bf16, gain_bf16):
    hidden_float = hidden_rows.astype(jnp.float32)
    inverse_rms = lax.rsqrt(
        jnp.mean(hidden_float * hidden_float, axis=1, keepdims=True) + norm_epsilon
    )
    normed = hidden_float * inverse_rms
    scaled = (normed * gain_bf16.astype(jnp.float32)).astype(jnp.bfloat16)
    key_latent = rotate_back(grad_rows, segment_row)
    weight_grad = lax.dot_general(
        scaled, key_latent, (((0,), (0,)), ((), ())), preferred_element_type=jnp.float32
    )
    input_grad = lax.dot_general(
        key_latent, weight_bf16, (((1,), (1,)), ((), ())), preferred_element_type=jnp.float32
    )
    gain_grad = jnp.sum(input_grad * normed, axis=0)
    return (weight_grad, gain_grad)


def adamw(master, first, second, gradient, decay):
    first_new = beta_one * first + (1.0 - beta_one) * gradient
    second_new = beta_two * second + (1.0 - beta_two) * gradient * gradient
    correct_one = 1.0 - beta_one ** (STEP + 1)
    correct_two = 1.0 - beta_two ** (STEP + 1)
    direction = first_new / correct_one / (jnp.sqrt(second_new / correct_two) + adam_epsilon)
    master_new = master - learning_rate * (direction + decay * master)
    return (master_new, first_new, second_new)


def shards(
    hidden,
    segment_ids,
    key_grad,
    weight_bf16,
    gain_bf16,
    weight_master,
    weight_first,
    weight_second,
    gain_master,
    gain_first,
    gain_second,
):
    weight_grad, gain_grad = local_terms(hidden, segment_ids[0], key_grad, weight_bf16, gain_bf16)
    outer_count = lax.axis_size("outer")
    inner_count = lax.axis_size("inner")
    model_width = weight_grad.shape[0]
    columns = weight_grad.shape[1]
    owned_rows = model_width // (outer_count * inner_count)
    weight_parts = weight_grad.reshape(outer_count, inner_count, owned_rows, columns)
    gain_parts = gain_grad.reshape(outer_count, inner_count, owned_rows)
    weight_parts, gain_parts = (
        lax.psum_scatter(
            weight_parts.astype(jnp.bfloat16), "inner", scatter_dimension=1, tiled=True
        ).astype(jnp.float32),
        lax.psum_scatter(
            gain_parts.astype(jnp.bfloat16), "inner", scatter_dimension=1, tiled=True
        ).astype(jnp.float32),
    )
    weight_parts, gain_parts = (
        lax.psum_scatter(weight_parts, "outer", scatter_dimension=0, tiled=True),
        lax.psum_scatter(gain_parts, "outer", scatter_dimension=0, tiled=True),
    )
    weight_summed = weight_parts.reshape(owned_rows, columns)
    gain_summed = gain_parts.reshape(owned_rows)
    weight_master_new, weight_first_new, weight_second_new = adamw(
        weight_master, weight_first, weight_second, weight_summed, 0.1
    )
    gain_master_new, gain_first_new, gain_second_new = adamw(
        gain_master, gain_first, gain_second, gain_summed, 0.0
    )
    lowered_weight = weight_master_new.astype(jnp.bfloat16)
    lowered_gain = gain_master_new.astype(jnp.bfloat16)
    weight_pieces = lowered_weight.reshape(1, 1, owned_rows, columns)
    gain_pieces = lowered_gain.reshape(1, 1, owned_rows)
    weight_pieces, gain_pieces = (
        lax.all_gather(weight_pieces, "outer", axis=0, tiled=True),
        lax.all_gather(gain_pieces, "outer", axis=0, tiled=True),
    )
    weight_pieces, gain_pieces = (
        lax.all_gather(weight_pieces, "inner", axis=1, tiled=True),
        lax.all_gather(gain_pieces, "inner", axis=1, tiled=True),
    )
    weight_bf16_new = weight_pieces.reshape(model_width, columns)
    gain_bf16_new = gain_pieces.reshape(model_width)
    return (
        weight_master_new,
        weight_first_new,
        weight_second_new,
        gain_master_new,
        gain_first_new,
        gain_second_new,
        weight_bf16_new,
        gain_bf16_new,
    )


def solution(mesh):
    return jax.shard_map(
        shards,
        mesh=mesh,
        in_specs=(
            P(("outer", "inner"), None),
            P(("outer", "inner"), None),
            P(("outer", "inner"), None),
            P(),
            P(),
            P(("outer", "inner"), None),
            P(("outer", "inner"), None),
            P(("outer", "inner"), None),
            P(("outer", "inner")),
            P(("outer", "inner")),
            P(("outer", "inner")),
        ),
        out_specs=(
            P(("outer", "inner"), None),
            P(("outer", "inner"), None),
            P(("outer", "inner"), None),
            P(("outer", "inner")),
            P(("outer", "inner")),
            P(("outer", "inner")),
            P(),
            P(),
        ),
        check_vma=False,
    )
```

profile of v0, /device:TPU:1, one launch (start us, length us, event | category | flops | bytes accessed | tf_op | source)
XLA Modules:
  0.0 1691.4 jit_solution(12654874229015328055)
XLA Ops:
  7.2 0.0 copy-start
  7.2 0.0 copy-start.3
  7.2 0.0 copy-start.2
  7.2 0.0 reduce-scatter.2.cloned.1.call-start
  7.2 0.0 copy-start.1
  7.3 1.0 select_reduce_fusion
  8.3 2.8 fusion.2
  11.1 0.0 copy-done.3
  11.1 0.0 copy-done.2
  11.1 0.2 fusion.12
  11.3 0.0 copy-done.1
  11.4 1.2 convolution_convert_fusion
  12.5 1.7 copy.35
  14.2 2.8 convert_element_type.54
  17.0 2.6 copy.36
  19.6 0.0 reduce-scatter.2.cloned.1.call-update
  19.6 0.0 all-reduce.6.cloned.1.call-start
  19.7 0.0 copy-done
  19.7 0.0 copy-start.7
  19.7 0.0 copy-start.8
  19.7 0.0 copy-start.9
  19.8 0.0 copy-start.4
  19.8 0.0 copy-start.5
  19.8 0.0 copy-start.6
  19.8 3.1 fusion.6
  22.9 0.4 convert_element_type.57
  23.3 0.3 copy.38
  23.6 1.3 dynamic-slice.3
  24.9 154.6 %all-reduce.2 = bf16[64,16,7]{0,2,1:T(8,128)(2,1)S(1)} all-reduce(bf16[64,16,7]{0,2,1:T(8,128)(2,1)S(1)} %copy.38), channel_id=6, replica_groups=mesh['outer'=64,'inner'=16] {'inner'}, use_global_device_ids=true, to_apply=%region_5.6.clone | all-reduce | flops 7168 | bytes 28672
  179.5 0.7 dynamic-slice_convert_fusion
  180.2 0.1 copy.39
  180.3 1.3 fusion.25
  181.6 413.0 %all-reduce.3 = f32[64,1,7]{2,1,0:T(1,128)S(1)} all-reduce(f32[64,1,7]{2,1,0:T(1,128)S(1)} %copy.39), channel_id=7, replica_groups=mesh['outer'=64,'inner'=16] {'outer'}, use_global_device_ids=true, to_apply=%region_6.7.clone | all-reduce | flops 448 | bytes 3584
  594.6 0.0 reduce-scatter.2.cloned.1.call-done
  594.6 1.8 copy.37
  596.3 0.0 all-reduce.6.cloned.1.call-update
  596.4 0.0 copy-done.7
  596.4 0.0 copy-done.8
  596.4 0.0 copy-done.9
  596.4 1.2 fusion.21
  598.2 0.2 dynamic-update-slice
  598.5 220.9 %all-reduce = bf16[448]{0:T(512)(128)(2,1)S(1)} all-reduce(bf16[448]{0:T(512)(128)(2,1)S(1)} %dynamic-update-slice), channel_id=3, replica_groups=mesh['outer'=64,'inner'=16] {'outer'}, use_global_device_ids=true, to_apply=%add | all-reduce | flops 448 | bytes 1792
  819.4 0.1 reshape.68
  819.5 0.1 copy.42
  819.6 66.7 %all_gather.15 = bf16[64,16,7]{0,2,1:T(8,128)(2,1)S(1)} all-gather(bf16[64,1,7]{0,2,1:T(8,128)(2,1)S(1)} %copy.42), channel_id=1, replica_groups=mesh['outer'=64,'inner'=16] {'inner'}, dimensions={1}, use_global_device_ids=true | all-gather | bytes 15232 | tf_op jit(solution)/shard_map/all_gather | solution.py:118
  886.2 0.3 copy.43
  886.5 1.0 reshape.66
  887.5 507.6 %all-reduce.6.cloned.1.call-done = f32[64,1,7,64]{3,1,2,0:T(1,128)} async-done(((f32[64,1,7,64]{3,1,2,0:T(1,128)}), f32[64,1,7,64]{3,1,2,0:T(1,128)}) %all-reduce.6.cloned.1.call-update) | async-done | bytes 114704
  1395.1 1.3 constant_dynamic-slice_fusion.1
  1396.4 0.0 copy-done.4
  1396.4 0.0 copy-done.5
  1396.4 0.0 copy-done.6
  1396.4 0.6 convert_bitcast_fusion
  1397.1 123.2 %all-gather.2 = bf16[64,7,64]{2,1,0:T(8,128)(2,1)S(1)} all-gather(bf16[1,7,64]{2,1,0:T(8,128)(2,1)S(1)} %get-tuple-element.36), channel_id=2, replica_groups=mesh['outer'=64,'inner'=16] {'outer'}, dimensions={0}, use_global_device_ids=true | all-gather | bytes 58240 | tf_op jit(solution)/shard_map/all_gather | solution.py:113
  1520.2 158.7 %all_gather.13 = bf16[64,16,7,64]{3,0,2,1:T(8,128)(2,1)S(1)} all-gather(bf16[64,1,7,64]{3,0,2,1:T(8,128)(2,1)S(1)} %copy.40), channel_id=1, replica_groups=mesh['outer'=64,'inner'=16] {'inner'}, dimensions={1}, use_global_device_ids=true | all-gather | bytes 974848 | tf_op jit(solution)/shard_map/all_gather | solution.py:117
  1679.0 1.2 copy.41
  1680.2 1.8 reshape.64
  1682.0 2.5 copy.44
  (6 shorter events, 0.1 us)
Async XLA Ops:
  7.2 12.5 copy-start
  7.2 3.9 copy-start.3
  7.2 3.9 copy-start.2
  7.2 587.4 %reduce-scatter.2.cloned.1.call-start = ((), (), s32[]{:S(2)}) async-start(), calls=%async_computation.1 | async-start | bytes 1949696 | tf_op jit(solution)/shard_map/reduce_scatter | solution.py:89
  7.2 4.1 copy-start.1
  19.6 1375.4 %all-reduce.6.cloned.1.call-start = ((), (), s32[]{:S(2)}) async-start(), calls=%async_computation.2 | async-start | bytes 458752
  19.7 576.6 %copy-start.7 = (f32[7]{0:T(128)S(1)}, f32[7]{0:T(128)}, u32[]{:S(2)}) copy-start(f32[7]{0:T(128)} %param.19) | copy-start | bytes 88
  19.7 576.6 %copy-start.8 = (f32[7]{0:T(128)S(1)}, f32[7]{0:T(128)}, u32[]{:S(2)}) copy-start(f32[7]{0:T(128)} %param.20) | copy-start | bytes 88
  19.7 576.6 %copy-start.9 = (f32[7]{0:T(128)S(1)}, f32[7]{0:T(128)}, u32[]{:S(2)}) copy-start(f32[7]{0:T(128)} %param.21) | copy-start | bytes 88
  19.8 1376.7 %copy-start.4 = (f32[7,64]{1,0:T(8,128)S(1)}, f32[7,64]{1,0:T(8,128)}, u32[]{:S(2)}) copy-start(f32[7,64]{1,0:T(8,128)} %param.16) | copy-start | bytes 5380
  19.8 1376.7 %copy-start.5 = (f32[7,64]{1,0:T(8,128)S(1)}, f32[7,64]{1,0:T(8,128)}, u32[]{:S(2)}) copy-start(f32[7,64]{1,0:T(8,128)} %param.17) | copy-start | bytes 5380
  19.8 1376.7 %copy-start.6 = (f32[7,64]{1,0:T(8,128)S(1)}, f32[7,64]{1,0:T(8,128)}, u32[]{:S(2)}) copy-start(f32[7,64]{1,0:T(8,128)} %param.18) | copy-start | bytes 5380
Sparse Core Ops, SparseCore 0:
  19.8 230.0 reduce-scatter.1
  596.5 798.5 all-reduce.5
where the time goes:
time: 1710 us; the launch traced here: 1690 us
  blocking collectives  1140 us (67%)
  waiting for transfers between devices  508 us (30%)
  local copies, waits for them, and re-layouts  21 us (1%)
    unnamed x3, blocking collectives  788 us
    unnamed x3, waiting for transfers between devices  508 us
    all_gather x1, blocking collectives, shards(): lax.all_gather(weight_pieces, 'inner', axis=1, tiled=True)  159 us
    all_gather x1, blocking collectives, shards(): lax.all_gather(weight_pieces, 'outer', axis=0, tiled=True)  123 us
    all_gather x1, blocking collectives, shards(): lax.all_gather(gain_pieces, 'inner', axis=1, tiled=True)  66.7 us
  transfers between devices with their start and end apart: 2, of which 1 were waited for; matrix products, arithmetic and copies ran while one was open for 1% of the time, Pallas kernels for 0%

commit v1 on v0

v1 whole, which is shorter than its diff:
```python
import functools

import jax
import jax.numpy as jnp
import numpy as np
from jax import lax
from jax.experimental import pallas as pl
from jax.experimental.pallas import tpu as pltpu
from jax.sharding import PartitionSpec as P

STEP = 20
beta_one = 0.9
beta_two = 0.95
learning_rate = 0.00022
adam_epsilon = 1e-08
norm_epsilon = 1e-06

MESH = pl.DeviceIdType.MESH
F32 = jnp.float32
BF16 = jnp.bfloat16
ROPE = 64
HALF = ROPE // 2
OWN = 7
LANES = 128
BLOCK = OWN * LANES

NC, NX, NY, NZL, NZH = 2, 4, 4, 8, 4


def rotary_table():
    frequency = 10000.0 ** (-np.arange(HALF) / HALF)
    angles = frequency[:, None] * np.arange(LANES)[None, :]
    return np.concatenate([np.cos(angles), np.sin(angles)]).astype(np.float32)


def iota(shape, axis):
    return lax.broadcasted_iota(jnp.int32, shape, axis)


def look_up(table, index):
    rows = [
        jnp.take_along_axis(table[8 * i : 8 * i + 8], index, axis=1)
        for i in range(table.shape[0] // 8)
    ]
    return jnp.concatenate(rows, axis=0)


def pack_shard(weight_ref, gain_ref):
    gains = jnp.concatenate([gain_ref[...], jnp.zeros((1, ROPE - OWN), F32)], axis=1)
    rows = []
    for p in range(4):
        right = weight_ref[2 * p + 1 : 2 * p + 2, :] if p < 3 else gains
        rows.append(jnp.concatenate([weight_ref[2 * p : 2 * p + 1, :], right], axis=1))
    return rows


def grads_kernel(
    hidden_ref, seg_ref, key_ref, weight_ref, gain_ref, table_ref,
    wm_ref, wf_ref, ws_ref, gm_ref, gf_ref, gs_ref,
    packed_ref, shard_ref, squares, wide, segs, gains,
):
    tokens, width = hidden_ref.shape
    padded = 2 * LANES
    for a, (w, g) in enumerate(((wm_ref, gm_ref), (wf_ref, gf_ref), (ws_ref, gs_ref))):
        for p, row in enumerate(pack_shard(w, g)):
            shard_ref[4 * a + p : 4 * a + p + 1, :] = row
    shard_ref[12:16, :] = jnp.ones((4, LANES), F32)
    gains[...] = gain_ref[...].astype(F32)

    squares[tokens:, :] = jnp.zeros((padded - tokens, LANES), F32)
    step = 48

    def square(i, carry):
        rows = pl.ds(pl.multiple_of(i * step, 16), step)
        total = jnp.zeros((step, LANES), F32)
        for j in range(width // LANES):
            h = hidden_ref[rows, j * LANES : (j + 1) * LANES].astype(F32)
            total = total + h * h
        squares[rows, :] = total
        return carry

    lax.fori_loop(0, tokens // step, square, 0)
    mean = jnp.sum(squares[...].T, axis=0, keepdims=True) * (1.0 / width)
    inverse_rms = lax.rsqrt(mean + norm_epsilon)[:, :tokens]

    segs[...] = jnp.full((8, padded), -1, jnp.int32)
    segs[:, :tokens] = jnp.broadcast_to(seg_ref[...], (8, tokens))
    ids = segs[...]
    lane = iota((8, padded), 1)
    begins = jnp.logical_or(ids != pltpu.roll(ids, 1, axis=1), lane == 0)
    start = jnp.where(begins, lane, 0)
    shift = 1
    while shift < padded:
        before = pltpu.roll(start, shift, axis=1)
        start = jnp.maximum(start, jnp.where(lane >= shift, before, 0))
        shift *= 2
    place = jnp.clip(lane - start, 0, LANES - 1)
    halves = [
        look_up(table_ref[...], place[:, i * LANES : (i + 1) * LANES]) for i in range(2)
    ]
    table = jnp.concatenate(halves, axis=1)[:, :tokens]
    cosine, sine = table[:HALF], table[HALF:]
    key = key_ref[...].astype(F32)
    a, b = key[:HALF], key[HALF:]
    latent = jnp.concatenate([a * cosine + b * sine, b * cosine - a * sine], axis=0)
    latent = latent.astype(BF16).astype(F32) * inverse_rms
    high = latent.astype(BF16)
    low = (latent - high.astype(F32)).astype(BF16)
    both = jnp.concatenate([high, low], axis=0)

    row8 = iota((8, LANES), 0)
    lane8 = iota((8, LANES), 1)
    left = iota((LANES, LANES), 1) < ROPE
    upper = iota((16, 8, LANES), 1) < 4
    for k in range(width // BLOCK):
        product = jnp.dot(
            both, hidden_ref[:, k * BLOCK : (k + 1) * BLOCK], preferred_element_type=F32
        )
        product = product[:ROPE] + product[ROPE:]
        for i in range(OWN):
            at = OWN * k + i
            part = product[:, i * LANES : (i + 1) * LANES]
            w = weight_ref[:, at * LANES : (at + 1) * LANES].astype(F32)
            gain_grad = jnp.sum(w * part, axis=0, keepdims=True)
            chosen = row8 == lax.rem(lane8 + i * LANES, OWN)
            block = jnp.concatenate(
                [
                    part * gains[at : at + 1, :],
                    jnp.where(chosen, gain_grad, 0.0),
                    jnp.zeros((LANES - ROPE - 8, LANES), F32),
                ],
                axis=0,
            )
            wide[k % 2, i * LANES : (i + 1) * LANES, :] = block.T
        rows = [wide[k % 2, pl.ds(r, LANES, stride=OWN), :] for r in range(OWN)]
        total = rows[0]
        for r in range(1, OWN):
            total = total + rows[r]
        tiles = [
            jnp.where(left, rows[2 * p], pltpu.roll(rows[2 * p + 1], ROPE, axis=1))
            for p in range(3)
        ]
        tiles.append(jnp.where(left, rows[6], total))
        tiles = [t.reshape(16, 8, LANES) for t in tiles]
        even, odd = [], []
        for one, two in ((tiles[0], tiles[1]), (tiles[2], tiles[3])):
            even.append(jnp.where(upper, one, pltpu.roll(two, 4, axis=1)))
            odd.append(jnp.where(upper, pltpu.roll(one, 4, axis=1), two))
        even = jnp.concatenate(even, axis=1).astype(BF16)
        odd = jnp.concatenate(odd, axis=1).astype(BF16)
        for q in range(16):
            x, core, y = q // 4, (q // 2) % 2, 2 * (q % 2)
            packed_ref[core, x, y, k] = even[q]
            packed_ref[core, x, y + 1, k] = odd[q]


def adamw(master, first, second, gradient, decay):
    first_new = beta_one * first + (1.0 - beta_one) * gradient
    second_new = beta_two * second + (1.0 - beta_two) * gradient * gradient
    correct_one = 1.0 - beta_one ** (STEP + 1)
    correct_two = 1.0 - beta_two ** (STEP + 1)
    direction = first_new / correct_one / (jnp.sqrt(second_new / correct_two) + adam_epsilon)
    master_new = master - learning_rate * (direction + decay * master)
    return (master_new, first_new, second_new)


def exchange_kernel(
    dims, packed_ref, shard_ref, gathered_ref, adam_ref,
    r1, sb, r2, zb, r3, hb, r4, shards, masters,
    s1, t1, s2, t2, s3, t3, s4, t4, s5, t5, s6, t6, s7, t7, s8, t8,
):
    nx, ny, nzl, nzh = dims
    outer, inner = lax.axis_index("outer"), lax.axis_index("inner")
    core, x, zl = lax.rem(outer, NC), lax.rem(outer // NC, nx), outer // (NC * nx)
    y, zh = inner // nzh, lax.rem(inner, nzh)

    def device(x=x, y=y, zl=zl, zh=zh, core=core):
        return ((zl * nx + x) * NC + core, y * nzh + zh)

    def send(src, dst, s, t, to):
        copy = pltpu.make_async_remote_copy(
            src_ref=src, dst_ref=dst, send_sem=s, recv_sem=t, device_id=to, device_id_type=MESH
        )
        copy.start()
        return copy

    sibling = device(core=1 - core)
    plane = [(dx, dy) for dx in range(nx) for dy in range(ny)]
    others = plane[1:]
    ahead = {o: (lax.rem(x + o[0], nx), lax.rem(y + o[1], ny)) for o in plane}
    behind = {o: (lax.rem(x + nx - o[0], nx), lax.rem(y + ny - o[1], ny)) for o in plane}
    up_lo = [lax.rem(zl + d, nzl) for d in range(nzl)]
    up_hi = [lax.rem(zh + d, nzh) for d in range(nzh)]

    barrier = pltpu.get_barrier_semaphore()
    peers = [sibling]
    peers += [device(x=ahead[o][0], y=ahead[o][1]) for o in others]
    peers += [device(zl=z) for z in up_lo[1:]]
    peers += [device(zh=z) for z in up_hi[1:]]
    for peer in peers:
        pl.semaphore_signal(barrier, inc=1, device_id=peer, device_id_type=MESH)
    pl.semaphore_wait(barrier, len(peers))

    first = [
        send(packed_ref.at[1 - core, ahead[dx, 0][0]], r1.at[dx], s1.at[dx], t1.at[dx], sibling)
        for dx in range(nx)
    ]
    swaps = [
        send(shard_ref, shards.at[zh], s8.at[d], t8.at[d], device(zh=up_hi[d]))
        for d in range(1, nzh)
    ]
    shards[zh] = shard_ref[...]

    second = []
    for dx in range(nx):
        xs = ahead[dx, 0][0]
        first[dx].wait_recv()
        sb[xs] = (packed_ref[core, xs].astype(F32) + r1[dx].astype(F32)).astype(BF16)
        for dy in range(ny):
            o = dx, dy
            if o == (0, 0):
                continue
            ys = ahead[o][1]
            slot = dx * ny + dy - 1
            second.append(send(sb.at[xs, ys], r2.at[slot], s2.at[slot], t2.at[slot], device(x=xs, y=ys)))

    for c in swaps:
        c.wait_recv()
    for a in range(3):
        for h in range(nzh):
            for p in range(4):
                masters[a, p * nzh + h : p * nzh + h + 1, :] = shards[h, 4 * a + p : 4 * a + p + 1, :]

    total = sb[x, y].astype(F32)
    for slot in range(len(others)):
        second[slot].wait_recv()
        total = total + r2[slot].astype(F32)
    zb[...] = total.astype(BF16)

    third = [
        send(zb.at[up_lo[d]], r3.at[d], s3.at[d], t3.at[d], device(zl=up_lo[d]))
        for d in range(1, nzl)
    ]
    total = zb[zl].astype(F32)
    for c, d in zip(third, range(1, nzl)):
        c.wait_recv()
        total = total + r3[d].astype(F32)
    hb[...] = total.astype(BF16)

    fourth = [
        send(hb, r4.at[zh], s4.at[d], t4.at[d], device(zh=up_hi[d])) for d in range(1, nzh)
    ]
    r4[zh] = hb[...]
    for c in fourth:
        c.wait_recv()
    gradient = r4[0].astype(F32)
    for h in range(1, nzh):
        gradient = gradient + r4[h].astype(F32)

    rows = 4 * nzh
    is_gain = jnp.logical_and(iota((rows, LANES), 0) >= 3 * nzh, iota((rows, LANES), 1) >= ROPE)
    decay = jnp.where(is_gain, 0.0, 0.1)
    new = adamw(masters[0], masters[1], masters[2], gradient, decay)
    for a in range(3):
        adam_ref[a] = new[a]

    own = gathered_ref.at[core, x, y]
    gathered_ref[core, x, y, zl] = new[0].astype(BF16)
    fifth = [
        send(own.at[zl], own.at[zl], s5.at[d], t5.at[d], device(zl=up_lo[d]))
        for d in range(1, nzl)
    ]
    for c in fifth:
        c.wait_recv()
    sixth = [
        send(own, own, s6.at[i], t6.at[i], device(x=ahead[o][0], y=ahead[o][1]))
        for i, o in enumerate(others)
    ]
    seventh = [send(own, own, s7.at[len(others)], t7.at[len(others)], sibling)]
    for i, o in enumerate(others):
        sixth[i].wait_recv()
        part = gathered_ref.at[core, behind[o][0], behind[o][1]]
        seventh.append(send(part, part, s7.at[i], t7.at[i], sibling))
    for c in seventh:
        c.wait_recv()
    for c in first + swaps + second + third + fourth + fifth + sixth + seventh:
        c.wait_send()


def unpack_kernel(
    nzh, gathered_ref, adam_ref, weight_ref, gain_ref, wm_ref, wf_ref, ws_ref, gm_ref, gf_ref, gs_ref, wide, gains
):
    zh = lax.rem(lax.axis_index("inner"), nzh)
    for a, (w, g) in enumerate(((wm_ref, gm_ref), (wf_ref, gf_ref), (ws_ref, gs_ref))):
        for p in range(4):
            row = adam_ref[a, pl.ds(p * nzh + zh, 1), :]
            w[2 * p : 2 * p + 1, :] = row[:, :ROPE]
            if p < 3:
                w[2 * p + 1 : 2 * p + 2, :] = row[:, ROPE:]
            else:
                g[...] = row[:, ROPE : ROPE + OWN]

    upper = iota((16, 8, LANES), 1) < 4
    lane = iota((LANES, LANES), 1)
    for k in range(gathered_ref.shape[3]):
        even, odd = [], []
        for q in range(16):
            x, core, y = q // 4, (q // 2) % 2, 2 * (q % 2)
            even.append(gathered_ref[core, x, y, k].astype(F32).reshape(1, 16, LANES))
            odd.append(gathered_ref[core, x, y + 1, k].astype(F32).reshape(1, 16, LANES))
        even, odd = jnp.concatenate(even, axis=0), jnp.concatenate(odd, axis=0)
        tiles = []
        for i in range(2):
            e, o = even[:, 8 * i : 8 * i + 8], odd[:, 8 * i : 8 * i + 8]
            tiles.append(jnp.where(upper, e, pltpu.roll(o, 4, axis=1)))
            tiles.append(jnp.where(upper, pltpu.roll(e, 4, axis=1), o))
        tiles = [t.reshape(LANES, LANES) for t in tiles]
        for r in range(OWN):
            tile = tiles[r // 2]
            if r % 2:
                tile = pltpu.roll(tile, ROPE, axis=1)
            gain = jnp.where(lane == ROPE + r, tiles[3], 0.0)
            wide[k % 2, pl.ds(r, LANES, stride=OWN), :] = jnp.where(lane < ROPE, tile, gain)
        for i in range(OWN):
            at = OWN * k + i
            block = wide[k % 2, i * LANES : (i + 1) * LANES, :].T
            weight_ref[:, at * LANES : (at + 1) * LANES] = block[:ROPE].astype(BF16)
            gains[at : at + 1, :] = jnp.sum(block[ROPE : ROPE + 8], axis=0, keepdims=True)
    gain_ref[...] = gains[...].astype(BF16)


def vmem():
    return pl.BlockSpec(memory_space=pltpu.VMEM)


def shapes(*items):
    return [jax.ShapeDtypeStruct(s, t) for s, t in items]


def local_gradients(hidden, segment_ids, key_t, weight_t, gain, states):
    tokens, width = hidden.shape
    return pl.pallas_call(
        grads_kernel,
        out_shape=shapes(((NC, NX, NY, NZL, 16, LANES), BF16), ((16, LANES), F32)),
        in_specs=[vmem()] * 12,
        out_specs=[vmem()] * 2,
        scratch_shapes=[
            pltpu.VMEM((2 * LANES, LANES), F32),
            pltpu.VMEM((2, BLOCK, LANES), F32),
            pltpu.VMEM((8, 2 * LANES), jnp.int32),
            pltpu.VMEM((width // LANES, LANES), F32),
        ],
        compiler_params=pltpu.CompilerParams(vmem_limit_bytes=40 * 1024 * 1024),
    )(hidden, segment_ids, key_t, weight_t, gain, jnp.asarray(rotary_table()), *states)


def exchange(dims, packed, shard):
    nx, ny, nzl, nzh = dims
    rows = 4 * nzh
    tile = (rows, LANES)
    dma = pltpu.SemaphoreType.DMA
    planes = nx * ny
    counts = [nx, planes, nzl, nzh, nzl, planes, planes, nzh]
    return pl.pallas_call(
        functools.partial(exchange_kernel, dims),
        out_shape=shapes(((NC, nx, ny, nzl, *tile), BF16), ((3, *tile), F32)),
        in_specs=[vmem()] * 2,
        out_specs=[vmem()] * 2,
        scratch_shapes=[
            pltpu.VMEM((nx, ny, nzl, *tile), BF16),
            pltpu.VMEM((nx, ny, nzl, *tile), BF16),
            pltpu.VMEM((planes - 1, nzl, *tile), BF16),
            pltpu.VMEM((nzl, *tile), BF16),
            pltpu.VMEM((nzl, *tile), BF16),
            pltpu.VMEM(tile, BF16),
            pltpu.VMEM((nzh, *tile), BF16),
            pltpu.VMEM((nzh, 16, LANES), F32),
            pltpu.VMEM((3, *tile), F32),
        ]
        + [dma((n,)) for n in counts for _ in range(2)],
        compiler_params=pltpu.CompilerParams(
            collective_id=0, has_side_effects=True, vmem_limit_bytes=40 * 1024 * 1024
        ),
    )(packed, shard)


def unpack(gathered, adam, width):
    own = [((OWN, ROPE), F32)] * 3 + [((1, OWN), F32)] * 3
    return pl.pallas_call(
        functools.partial(unpack_kernel, NZH),
        out_shape=shapes(((ROPE, width), BF16), ((width // LANES, LANES), BF16), *own),
        in_specs=[vmem()] * 2,
        out_specs=[vmem()] * 8,
        scratch_shapes=[
            pltpu.VMEM((2, BLOCK, LANES), F32),
            pltpu.VMEM((width // LANES, LANES), F32),
        ],
        compiler_params=pltpu.CompilerParams(vmem_limit_bytes=40 * 1024 * 1024),
    )(gathered, adam)


def shards(
    hidden, segment_ids, key_grad, weight_bf16, gain_bf16,
    weight_master, weight_first, weight_second, gain_master, gain_first, gain_second,
):
    width = hidden.shape[1]
    states = [weight_master, weight_first, weight_second]
    states += [g.reshape(1, OWN) for g in (gain_master, gain_first, gain_second)]
    packed, shard = local_gradients(
        hidden, segment_ids, key_grad.T, weight_bf16.T, gain_bf16.reshape(width // LANES, LANES), states
    )
    gathered, adam = exchange((NX, NY, NZL, NZH), packed, shard)
    weight_t, gain, wm, wf, ws, gm, gf, gs = unpack(gathered, adam, width)
    return (
        wm, wf, ws, gm.reshape(OWN), gf.reshape(OWN), gs.reshape(OWN), weight_t.T, gain.reshape(width)
    )


def solution(mesh):
    both = P(("outer", "inner"), None)
    one = P(("outer", "inner"))
    return jax.shard_map(
        shards,
        mesh=mesh,
        in_specs=(both, both, both, P(), P(), both, both, both, one, one, one),
        out_specs=(both, both, both, one, one, one, P(), P()),
        check_vma=False,
    )
```

time: 1710 us -> 94.8 us (0.06); the launches traced: 1690 us -> 94.3 us
  blocking collectives: 1140 us -> 0 us
  waiting for transfers between devices: 508 us -> 0 us
  Pallas kernels: 0 us -> 83.6 us
    unnamed x3 -> x0, blocking collectives: 788 us -> none
    unnamed x3 -> x0, waiting for transfers between devices: 508 us -> none
    all_gather x3 -> x0, blocking collectives: 349 us -> none  [the longest x1 159 us: shards(): lax.all_gather(weight_pieces, 'inner', axis=1, tiled=True)]
    pallas_call x0 -> x3, Pallas kernels: none -> 83.6 us  [the longest x1 77.6 us: exchange(): pl.pallas_call(functools.partial(exchange_kernel, dims), out_shape=shapes...]
  transfers between devices with their start and end apart: 2 -> 0, of which waited for: 1 -> 0; matrix products, arithmetic and copies ran while one was open for 1% -> 0% of each run, Pallas kernels for 0% -> 0%
where the time goes in v1:
time: 94.8 us; the launch traced here: 94.3 us
  Pallas kernels  83.6 us (88%)
  local copies, waits for them, and re-layouts  10.1 us (11%)
    pallas_call x1, Pallas kernels, exchange(): pl.pallas_call(functools.partial(exchange_kernel, dims), out_shape=shapes...  77.6 us
    unnamed x24, local copies, waits for them, and re-layouts  10.1 us
    pallas_call x1, Pallas kernels, local_gradients(): pl.pallas_call(grads_kernel, out_shape=shapes(((NC, NX, NY, NZL, 16, LANE...  3.64 us
    pallas_call x1, Pallas kernels, unpack(): pl.pallas_call(functools.partial(unpack_kernel, NZH), out_shape=shapes(((...  2.33 us

profile of v1, /device:TPU:1, one launch (start us, length us, event | category | flops | bytes accessed | tf_op | source)
XLA Modules:
  0.0 94.3 jit_solution(5852210138735025646)
XLA Ops:
  0.6 0.0 copy-start
  0.6 2.0 %copy-done = bf16[240,7168]{1,0:T(8,128)(2,1)S(1)} copy-done((bf16[240,7168]{1,0:T(8,128)(2,1)S(1)}, bf16[240,7168]{1,0:T(8,128)(2,1)}, u32[]{:S(2)}) %copy-start) | copy-done | bytes 3440664
  2.6 0.0 copy-start.1
  2.6 1.2 %copy-done.1 = bf16[7168,64]{0,1:T(8,128)(2,1)S(1)} copy-done((bf16[7168,64]{0,1:T(8,128)(2,1)S(1)}, bf16[7168,64]{0,1:T(8,128)(2,1)}, u32[]{:S(2)}) %copy-start.1) | copy-done | bytes 917528
  3.8 0.0 copy-start.2
  3.8 0.8 copy-done.2
  4.5 0.0 copy-start.3
  4.6 0.8 copy-done.3
  5.3 0.0 copy-start.4
  5.3 0.7 copy-done.4
  6.0 0.0 copy-start.5
  6.0 0.7 copy-done.5
  6.7 0.0 copy-start.6
  6.7 0.7 copy-done.6
  7.4 0.0 copy-start.7
  7.4 0.7 copy-done.7
  8.1 0.0 copy-start.8
  8.1 0.7 copy-done.8
  8.8 0.0 copy-start.9
  8.8 0.7 copy-done.9
  9.4 0.0 copy-start.10
  9.4 0.7 copy-done.10
  10.1 0.0 copy-start.11
  10.1 0.7 copy-done.11
  10.7 3.6 %shard_map.179 = (bf16[2,4,4,8,16,128]{5,4,3,2,1,0:T(8,128)(2,1)S(1)}, f32[16,128]{1,0:T(8,128)S(1)}) custom-call(bf16[240,7168]{1,0:T(8,128)(2,1)S(1)} %copy-done, s32[1,240]{1,0:T(1,128)S(1)} %copy-done.8, bf16[64,240]{1,0:T(8,128)(2,1)S(1)} %bitcast.12, bf16[64,7168]{1,0:T(8,128)(2,1)S(1)} %bitcast.11, bf16[56,128]{1,0:T(8,128)(2,1)S(1)} %bitcast.13, ...), custom_call_target="tpu_custom_call" | custom-call | tf_op jit(solution)/shard_map/pallas_call | solution.py:342
  14.4 77.6 %shard_map.180 = (bf16[2,4,4,8,16,128]{5,4,3,2,1,0:T(8,128)(2,1)S(1)}, f32[3,16,128]{2,1,0:T(8,128)S(1)}) custom-call(bf16[2,4,4,8,16,128]{5,4,3,2,1,0:T(8,128)(2,1)S(1)} %get-tuple-element.20.packed_ref, f32[16,128]{1,0:T(8,128)S(1)} %get-tuple-element.21.shard_ref), custom_call_target="tpu_custom_call" | custom-call | tf_op jit(solution)/shard_map/pallas_call | solution.py:364
  92.0 2.3 %shard_map.181 = (bf16[64,7168]{1,0:T(8,128)(2,1)}, bf16[56,128]{1,0:T(8,128)(2,1)}, f32[7,64]{1,0:T(8,128)}, f32[7,64]{1,0:T(8,128)}, f32[7,64]{1,0:T(8,128)}, ...) custom-call(bf16[2,4,4,8,16,128]{5,4,3,2,1,0:T(8,128)(2,1)S(1)} %get-tuple-element.22.gathered_ref, ...), custom_call_target="tpu_custom_call" | custom-call | tf_op jit(solution)/shard_map/pallas_call | solution.py:389
Async XLA Ops:
  0.6 2.0 %copy-start = (bf16[240,7168]{1,0:T(8,128)(2,1)S(1)}, bf16[240,7168]{1,0:T(8,128)(2,1)}, u32[]{:S(2)}) copy-start(bf16[240,7168]{1,0:T(8,128)(2,1)} %hidden_ref.1) | copy-start | bytes 10321924
  2.6 1.2 %copy-start.1 = (bf16[7168,64]{0,1:T(8,128)(2,1)S(1)}, bf16[7168,64]{0,1:T(8,128)(2,1)}, u32[]{:S(2)}) copy-start(bf16[7168,64]{0,1:T(8,128)(2,1)} %param.15) | copy-start | bytes 2752516
  3.8 0.8 copy-start.2
  4.5 0.8 copy-start.3
  5.3 0.7 copy-start.4
  6.0 0.7 copy-start.5
  6.7 0.7 copy-start.6
  7.4 0.7 copy-start.7
  8.1 0.7 copy-start.8
  8.8 0.7 copy-start.9
  9.4 0.7 copy-start.10
  10.1 0.7 copy-start.11

commit v2 on v1

v2 whole, which is shorter than its diff:
```python
import jax
import jax.numpy as jnp
import numpy as np
from jax import lax
from jax.experimental import pallas as pl
from jax.experimental.pallas import tpu as pltpu
from jax.sharding import PartitionSpec as P

STEP = 20
beta_one = 0.9
beta_two = 0.95
learning_rate = 0.00022
adam_epsilon = 1e-08
norm_epsilon = 1e-06

MESH = pl.DeviceIdType.MESH
F32 = jnp.float32
BF16 = jnp.bfloat16
ROPE = 64
HALF = ROPE // 2
OWN = 7
LANES = 128
BLOCK = OWN * LANES

NC, NX, NY, NZL, NZH = 2, 4, 4, 8, 4
NEAR = 4
FAR = NZL * NZH // NEAR
SPAN = NZL // NEAR
ROWS = 48


def rotary_table():
    frequency = 10000.0 ** (-np.arange(HALF) / HALF)
    angles = frequency[:, None] * np.arange(LANES)[None, :]
    return np.concatenate([np.cos(angles), np.sin(angles)]).astype(np.float32)


def iota(shape, axis):
    return lax.broadcasted_iota(jnp.int32, shape, axis)


def look_up(table, index):
    rows = [
        jnp.take_along_axis(table[8 * i : 8 * i + 8], index, axis=1)
        for i in range(table.shape[0] // 8)
    ]
    return jnp.concatenate(rows, axis=0)


def pack_shard(states):
    weight_ref, gain_ref = states
    gains = jnp.concatenate([gain_ref[...], jnp.zeros((1, ROPE - OWN), F32)], axis=1)
    rows = []
    for p in range(4):
        right = weight_ref[2 * p + 1 : 2 * p + 2, :] if p < 3 else gains
        rows.append(jnp.concatenate([weight_ref[2 * p : 2 * p + 1, :], right], axis=1))
    return rows


def latent_pair(seg_ref, key_ref, table_ref, segs, inverse_rms, tokens):
    padded = 2 * LANES
    segs[...] = jnp.full((8, padded), -1, jnp.int32)
    segs[:, :tokens] = jnp.broadcast_to(seg_ref[...], (8, tokens))
    ids = segs[...]
    lane = iota((8, padded), 1)
    begins = jnp.logical_or(ids != pltpu.roll(ids, 1, axis=1), lane == 0)
    start = jnp.where(begins, lane, 0)
    shift = 1
    while shift < padded:
        before = pltpu.roll(start, shift, axis=1)
        start = jnp.maximum(start, jnp.where(lane >= shift, before, 0))
        shift *= 2
    place = jnp.clip(lane - start, 0, LANES - 1)
    halves = [
        look_up(table_ref[...], place[:, i * LANES : (i + 1) * LANES]) for i in range(2)
    ]
    table = jnp.concatenate(halves, axis=1)[:, :tokens]
    cosine, sine = table[:HALF], table[HALF:]
    key = key_ref[...].astype(F32)
    a, b = key[:HALF], key[HALF:]
    latent = jnp.concatenate([a * cosine + b * sine, b * cosine - a * sine], axis=0)
    latent = latent.astype(BF16).astype(F32) * inverse_rms()
    high = latent.astype(BF16)
    low = (latent - high.astype(F32)).astype(BF16)
    return jnp.concatenate([high, low], axis=0)


def gradient_block(both, hidden, weight, gain_rows, wide):
    row8 = iota((8, LANES), 0)
    lane8 = iota((8, LANES), 1)
    left = iota((LANES, LANES), 1) < ROPE
    upper = iota((16, 8, LANES), 1) < 4
    product = jnp.dot(both, hidden, preferred_element_type=F32)
    product = product[:ROPE] + product[ROPE:]
    for i in range(OWN):
        part = product[:, i * LANES : (i + 1) * LANES]
        w = weight[:, i * LANES : (i + 1) * LANES].astype(F32)
        gain_grad = jnp.sum(w * part, axis=0, keepdims=True)
        chosen = row8 == lax.rem(lane8 + i * LANES, OWN)
        block = jnp.concatenate(
            [
                part * gain_rows(i),
                jnp.where(chosen, gain_grad, 0.0),
                jnp.zeros((LANES - ROPE - 8, LANES), F32),
            ],
            axis=0,
        )
        wide[i * LANES : (i + 1) * LANES, :] = block.T
    rows = [wide[pl.ds(r, LANES, stride=OWN), :] for r in range(OWN)]
    total = rows[0]
    for r in range(1, OWN):
        total = total + rows[r]
    tiles = [
        jnp.where(left, rows[2 * p], pltpu.roll(rows[2 * p + 1], ROPE, axis=1))
        for p in range(3)
    ]
    tiles.append(jnp.where(left, rows[6], total))
    tiles = [t.reshape(16, 8, LANES) for t in tiles]
    even, odd = [], []
    for one, two in ((tiles[0], tiles[1]), (tiles[2], tiles[3])):
        even.append(jnp.where(upper, one, pltpu.roll(two, 4, axis=1)))
        odd.append(jnp.where(upper, pltpu.roll(one, 4, axis=1), two))
    even = jnp.concatenate(even, axis=1).astype(BF16)
    odd = jnp.concatenate(odd, axis=1).astype(BF16)
    return even, odd


def adamw(master, first, second, gradient, decay):
    first_new = beta_one * first + (1.0 - beta_one) * gradient
    second_new = beta_two * second + (1.0 - beta_two) * gradient * gradient
    correct_one = 1.0 - beta_one ** (STEP + 1)
    correct_two = 1.0 - beta_two ** (STEP + 1)
    direction = first_new / correct_one / (jnp.sqrt(second_new / correct_two) + adam_epsilon)
    master_new = master - learning_rate * (direction + decay * master)
    return (master_new, first_new, second_new)


def step_kernel(
    hidden_hbm, seg_hbm, key_hbm, weight_hbm, gain_hbm, table_hbm,
    wm_hbm, wf_hbm, ws_hbm, gm_hbm, gf_hbm, gs_hbm,
    gathered_ref, adam_ref,
    hidden_ref, seg_ref, key_ref, weight_ref, gain_ref, table_ref,
    wm_ref, wf_ref, ws_ref, gm_ref, gf_ref, gs_ref,
    squares, wide, segs, gains, packed_ref, shard_ref,
    r1, sb, r2, zb, r3, hb, r4, shards, masters, in_sem, row_sem,
    s1, t1, s2, t2, s3, t3, s4, t4, s5, t5, s6, t6, s7, t7, s8, t8,
):
    tokens, width = hidden_ref.shape
    parts = tokens // ROWS
    outer, inner = lax.axis_index("outer"), lax.axis_index("inner")
    core, x = lax.rem(outer, NC), lax.rem(outer // NC, NX)
    y, z = inner // NZH, lax.rem(inner, NZH) * NZL + outer // (NC * NX)
    near, far = lax.rem(z, NEAR), z // NEAR

    def device(x=x, y=y, near=near, far=far, core=core):
        z = far * NEAR + near
        return ((lax.rem(z, NZL) * NX + x) * NC + core, y * NZH + z // NZL)

    loads = [
        pltpu.make_async_copy(src, dst, in_sem.at[i])
        for i, (src, dst) in enumerate(
            (
                (seg_hbm, seg_ref), (key_hbm, key_ref), (table_hbm, table_ref),
                (gain_hbm, gain_ref), (weight_hbm, weight_ref),
                (wm_hbm, wm_ref), (wf_hbm, wf_ref), (ws_hbm, ws_ref),
                (gm_hbm, gm_ref), (gf_hbm, gf_ref), (gs_hbm, gs_ref),
            )
        )
    ]

    def part_of_hidden(i):
        rows = pl.ds(pl.multiple_of(i * ROWS, 16), ROWS)
        return pltpu.make_async_copy(hidden_hbm.at[rows], hidden_ref.at[rows], row_sem.at[i])

    for load in loads[:4]:
        load.start()
    for i in range(parts):
        part_of_hidden(i).start()
    for load in loads[4:]:
        load.start()

    sibling = device(core=1 - core)
    plane = [(dx, dy) for dx in range(NX) for dy in range(NY)]
    others = plane[1:]
    ahead = {o: (lax.rem(x + o[0], NX), lax.rem(y + o[1], NY)) for o in plane}
    behind = {o: (lax.rem(x + NX - o[0], NX), lax.rem(y + NY - o[1], NY)) for o in plane}
    up_near = [lax.rem(near + d, NEAR) for d in range(NEAR)]
    up_far = [lax.rem(far + d, FAR) for d in range(FAR)]
    far_first = sorted(range(1, FAR), key=lambda d: -min(d, FAR - d))

    barrier = pltpu.get_barrier_semaphore()
    peers = [device(far=up_far[d]) for d in far_first]
    peers += [device(near=n) for n in up_near[1:]]
    peers += [device(x=ahead[o][0], y=ahead[o][1]) for o in others]
    peers += [sibling]
    for peer in peers:
        pl.semaphore_signal(barrier, inc=1, device_id=peer, device_id_type=MESH)

    def send(src, dst, s, t, to):
        copy = pltpu.make_async_remote_copy(
            src_ref=src, dst_ref=dst, send_sem=s, recv_sem=t, device_id=to, device_id_type=MESH
        )
        copy.start()
        return copy

    squares[tokens:, :] = jnp.zeros((2 * LANES - tokens, LANES), F32)

    def square(i, carry):
        part_of_hidden(i).wait()
        rows = pl.ds(pl.multiple_of(i * ROWS, 16), ROWS)
        total = jnp.zeros((ROWS, LANES), F32)
        for j in range(width // LANES):
            h = hidden_ref[rows, j * LANES : (j + 1) * LANES].astype(F32)
            total = total + h * h
        squares[rows, :] = total
        return carry

    def inverse_rms():
        lax.fori_loop(0, parts, square, 0)
        mean = jnp.sum(squares[...].T, axis=0, keepdims=True) * (1.0 / width)
        return lax.rsqrt(mean + norm_epsilon)[:, :tokens]

    for load in loads[:3]:
        load.wait()
    both = latent_pair(seg_ref, key_ref, table_ref, segs, inverse_rms, tokens)
    for load in loads[3:5]:
        load.wait()
    gains[...] = gain_ref[...].astype(F32)

    def block(k, carry):
        columns = pl.ds(pl.multiple_of(k * BLOCK, LANES), BLOCK)
        even, odd = gradient_block(
            both, hidden_ref[:, columns], weight_ref[:, columns],
            lambda i: gains[pl.ds(OWN * k + i, 1), :], wide,
        )
        n, h = lax.rem(k, NEAR), k // NEAR
        for q in range(16):
            xq, cq, yq = q // 4, (q // 2) % 2, 2 * (q % 2)
            packed_ref[cq, xq, yq, n, h] = even[q]
            packed_ref[cq, xq, yq + 1, n, h] = odd[q]
        return carry

    lax.fori_loop(0, width // BLOCK, block, 0)

    for load in loads[5:]:
        load.wait()
    for a, states in enumerate(((wm_ref, gm_ref), (wf_ref, gf_ref), (ws_ref, gs_ref))):
        for p, row in enumerate(pack_shard(states)):
            shard_ref[4 * a + p : 4 * a + p + 1, :] = row
    shard_ref[12:16, :] = jnp.ones((4, LANES), F32)

    pl.semaphore_wait(barrier, len(peers))

    first = [
        send(packed_ref.at[1 - core, ahead[dx, 0][0]], r1.at[dx], s1.at[dx], t1.at[dx], sibling)
        for dx in range(NX)
    ]
    swaps = [
        send(shard_ref, shards.at[far], s8.at[d], t8.at[d], device(far=up_far[d]))
        for d in far_first
    ]
    shards[far] = shard_ref[...]

    second = []
    for dx in range(NX):
        xs = ahead[dx, 0][0]
        first[dx].wait_recv()
        sb[xs] = (packed_ref[core, xs].astype(F32) + r1[dx].astype(F32)).astype(BF16)
        for dy in range(NY):
            o = dx, dy
            if o == (0, 0):
                continue
            ys = ahead[o][1]
            slot = dx * NY + dy - 1
            second.append(send(sb.at[xs, ys], r2.at[slot], s2.at[slot], t2.at[slot], device(x=xs, y=ys)))

    total = sb[x, y].astype(F32)
    for slot in range(len(others)):
        second[slot].wait_recv()
        total = total + r2[slot].astype(F32)
    zb[...] = total.astype(BF16)

    third = [
        send(zb.at[up_near[d]], r3.at[d], s3.at[d], t3.at[d], device(near=up_near[d]))
        for d in range(1, NEAR)
    ]

    for c in swaps:
        c.wait_recv()
    for a in range(3):
        for f in range(FAR):
            for p in range(4):
                row = p * NZH + f // SPAN
                masters[a, f % SPAN, row : row + 1, :] = shards[f, 4 * a + p : 4 * a + p + 1, :]

    total = zb[near].astype(F32)
    for c, d in zip(third, range(1, NEAR)):
        c.wait_recv()
        total = total + r3[d].astype(F32)
    hb[...] = total.astype(BF16)

    fourth = [
        send(hb, r4.at[far], s4.at[d], t4.at[d], device(far=up_far[d])) for d in far_first
    ]
    r4[far] = hb[...]
    for c in fourth:
        c.wait_recv()
    gradient = r4[0].astype(F32)
    for f in range(1, FAR):
        gradient = gradient + r4[f].astype(F32)

    tile = gradient.shape
    is_gain = jnp.logical_and(iota(tile, 1) >= 3 * NZH, iota(tile, 2) >= ROPE)
    decay = jnp.where(is_gain, 0.0, 0.1)
    new = adamw(masters[0], masters[1], masters[2], gradient, decay)
    for a in range(3):
        adam_ref[a] = new[a]

    own = gathered_ref.at[core, x, y]
    gathered_ref[core, x, y, near] = new[0].astype(BF16)
    fifth = [
        send(own.at[near], own.at[near], s5.at[d], t5.at[d], device(near=up_near[d]))
        for d in range(1, NEAR)
    ]
    for c in fifth:
        c.wait_recv()
    sixth = [
        send(own, own, s6.at[i], t6.at[i], device(x=ahead[o][0], y=ahead[o][1]))
        for i, o in enumerate(others)
    ]
    seventh = [send(own, own, s7.at[len(others)], t7.at[len(others)], sibling)]
    for i, o in enumerate(others):
        sixth[i].wait_recv()
        part = gathered_ref.at[core, behind[o][0], behind[o][1]]
        seventh.append(send(part, part, s7.at[i], t7.at[i], sibling))
    for c in seventh:
        c.wait_recv()
    for c in first + swaps + second + third + fourth + fifth + sixth + seventh:
        c.wait_send()


def unpack_kernel(
    gathered_hbm, adam_hbm, weight_ref, gain_ref, wm_ref, wf_ref, ws_ref, gm_ref, gf_ref, gs_ref,
    gathered_ref, adam_ref, wide, gains, in_sem,
):
    loads = [
        pltpu.make_async_copy(
            gathered_hbm.at[:, :, :, n], gathered_ref.at[:, :, :, n], in_sem.at[n]
        )
        for n in range(NEAR)
    ]
    loads.append(pltpu.make_async_copy(adam_hbm, adam_ref, in_sem.at[NEAR]))
    for load in loads:
        load.start()
    upper = iota((16, 8, LANES), 1) < 4
    lane = iota((LANES, LANES), 1)
    for turn in range(NZL):
        n, h = turn // SPAN, turn % SPAN
        k = h * NEAR + n
        if h == 0:
            loads[n].wait()
        even, odd = [], []
        for q in range(16):
            x, core, y = q // 4, (q // 2) % 2, 2 * (q % 2)
            even.append(gathered_ref[core, x, y, n, h].astype(F32).reshape(1, 16, LANES))
            odd.append(gathered_ref[core, x, y + 1, n, h].astype(F32).reshape(1, 16, LANES))
        even, odd = jnp.concatenate(even, axis=0), jnp.concatenate(odd, axis=0)
        tiles = []
        for i in range(2):
            e, o = even[:, 8 * i : 8 * i + 8], odd[:, 8 * i : 8 * i + 8]
            tiles.append(jnp.where(upper, e, pltpu.roll(o, 4, axis=1)))
            tiles.append(jnp.where(upper, pltpu.roll(e, 4, axis=1), o))
        tiles = [t.reshape(LANES, LANES) for t in tiles]
        for r in range(OWN):
            tile = tiles[r // 2]
            if r % 2:
                tile = pltpu.roll(tile, ROPE, axis=1)
            gain = jnp.where(lane == ROPE + r, tiles[3], 0.0)
            wide[turn % 2, pl.ds(r, LANES, stride=OWN), :] = jnp.where(lane < ROPE, tile, gain)
        for i in range(OWN):
            at = OWN * k + i
            block = wide[turn % 2, i * LANES : (i + 1) * LANES, :].T
            weight_ref[:, at * LANES : (at + 1) * LANES] = block[:ROPE].astype(BF16)
            gains[at : at + 1, :] = jnp.sum(block[ROPE : ROPE + 8], axis=0, keepdims=True)
    gain_ref[...] = gains[...].astype(BF16)
    loads[NEAR].wait()
    zh = lax.rem(lax.axis_index("inner"), NZH)
    zl = lax.axis_index("outer") // (NC * NX)
    for a, (w, g) in enumerate(((wm_ref, gm_ref), (wf_ref, gf_ref), (ws_ref, gs_ref))):
        for p in range(4):
            row = adam_ref[a, zl // NEAR, pl.ds(p * NZH + zh, 1), :]
            w[2 * p : 2 * p + 1, :] = row[:, :ROPE]
            if p < 3:
                w[2 * p + 1 : 2 * p + 2, :] = row[:, ROPE:]
            else:
                g[...] = row[:, ROPE : ROPE + OWN]


def vmem():
    return pl.BlockSpec(memory_space=pltpu.VMEM)


def shapes(*items):
    return [jax.ShapeDtypeStruct(s, t) for s, t in items]


def step(operands):
    hidden = operands[0]
    tokens, width = hidden.shape
    dma = pltpu.SemaphoreType.DMA
    piece = (SPAN, 16, LANES)
    others = NX * NY - 1
    chunk = (NEAR, *piece)
    counts = [NX, others, NEAR, FAR, NEAR, others, others + 1, FAR]
    return pl.pallas_call(
        step_kernel,
        out_shape=shapes(((NC, NX, NY, *chunk), BF16), ((3, *piece), F32)),
        in_specs=[pl.BlockSpec(memory_space=pltpu.HBM)] * len(operands),
        out_specs=[vmem()] * 2,
        scratch_shapes=[pltpu.VMEM(o.shape, o.dtype) for o in operands]
        + [
            pltpu.VMEM((2 * LANES, LANES), F32),
            pltpu.VMEM((BLOCK, LANES), F32),
            pltpu.VMEM((8, 2 * LANES), jnp.int32),
            pltpu.VMEM((width // LANES, LANES), F32),
            pltpu.VMEM((NC, NX, NY, *chunk), BF16),
            pltpu.VMEM((16, LANES), F32),
            pltpu.VMEM((NX, NY, *chunk), BF16),
            pltpu.VMEM((NX, NY, *chunk), BF16),
            pltpu.VMEM((others, *chunk), BF16),
            pltpu.VMEM(chunk, BF16),
            pltpu.VMEM(chunk, BF16),
            pltpu.VMEM(piece, BF16),
            pltpu.VMEM((FAR, *piece), BF16),
            pltpu.VMEM((FAR, 16, LANES), F32),
            pltpu.VMEM((3, *piece), F32),
            dma((len(operands) - 1,)),
            dma((tokens // ROWS,)),
        ]
        + [dma((n,)) for n in counts for _ in range(2)],
        compiler_params=pltpu.CompilerParams(
            collective_id=0, has_side_effects=True, vmem_limit_bytes=56 * 1024 * 1024
        ),
    )(*operands)


def unpack(gathered, adam, width):
    own = [((OWN, ROPE), F32)] * 3 + [((1, OWN), F32)] * 3
    return pl.pallas_call(
        unpack_kernel,
        out_shape=shapes(((ROPE, width), BF16), ((width // LANES, LANES), BF16), *own),
        in_specs=[pl.BlockSpec(memory_space=pltpu.HBM)] * 2,
        out_specs=[vmem()] * 8,
        scratch_shapes=[
            pltpu.VMEM(gathered.shape, gathered.dtype),
            pltpu.VMEM(adam.shape, adam.dtype),
            pltpu.VMEM((2, BLOCK, LANES), F32),
            pltpu.VMEM((width // LANES, LANES), F32),
            pltpu.SemaphoreType.DMA((NEAR + 1,)),
        ],
        compiler_params=pltpu.CompilerParams(vmem_limit_bytes=56 * 1024 * 1024),
    )(gathered, adam)


def shards(
    hidden, segment_ids, key_grad, weight_bf16, gain_bf16,
    weight_master, weight_first, weight_second, gain_master, gain_first, gain_second,
):
    width = hidden.shape[1]
    states = [weight_master, weight_first, weight_second]
    states += [g.reshape(1, OWN) for g in (gain_master, gain_first, gain_second)]
    operands = [hidden, segment_ids, key_grad.T, weight_bf16.T, gain_bf16.reshape(width // LANES, LANES)]
    gathered, adam = step([*operands, jnp.asarray(rotary_table()), *states])
    weight_t, gain, wm, wf, ws, gm, gf, gs = unpack(gathered, adam, width)
    return (
        wm, wf, ws, gm.reshape(OWN), gf.reshape(OWN), gs.reshape(OWN), weight_t.T, gain.reshape(width)
    )


def solution(mesh):
    both = P(("outer", "inner"), None)
    one = P(("outer", "inner"))
    return jax.shard_map(
        shards,
        mesh=mesh,
        in_specs=(both, both, both, P(), P(), both, both, both, one, one, one),
        out_specs=(both, both, both, one, one, one, P(), P()),
        check_vma=False,
    )
```

time: 94.8 us -> 77 us (0.81)
  local copies, waits for them, and re-layouts: 10.1 us -> 0 us
  Pallas kernels: 83.6 us -> 76.2 us
    unnamed x24 -> x0, local copies, waits for them, and re-layouts: 10.1 us -> none
    pallas_call x3 -> x2, Pallas kernels: 83.6 us -> 76.2 us  [the longest x1 72.5 us: step(): pl.pallas_call(step_kernel, out_shape=shapes(((NC, NX, NY, *chunk), BF16)...]
where the time goes in v2:
time: 77 us; the launch traced here: 76.8 us
  Pallas kernels  76.2 us (99%)
    pallas_call x1, Pallas kernels, step(): pl.pallas_call(step_kernel, out_shape=shapes(((NC, NX, NY, *chunk), BF16)...  72.5 us
    pallas_call x1, Pallas kernels, unpack(): pl.pallas_call(unpack_kernel, out_shape=shapes(((ROPE, width), BF16), ((w...  3.72 us

profile of v2, /device:TPU:1, one launch (start us, length us, event | category | flops | bytes accessed | tf_op | source)
XLA Modules:
  0.0 76.8 jit_solution(438213593380746007)
XLA Ops:
  0.6 72.5 %shard_map.179 = (bf16[2,4,4,4,2,16,128]{6,5,4,3,2,1,0:T(8,128)(2,1)}, f32[3,2,16,128]{3,2,1,0:T(8,128)}) custom-call(bf16[240,7168]{1,0:T(8,128)(2,1)} %hidden_hbm.1, s32[1,240]{1,0:T(1,128)} %seg_hbm.1, bf16[64,240]{1,0:T(8,128)(2,1)} %bitcast.12, bf16[64,7168]{1,0:T(8,128)(2,1)} %bitcast.11, bf16[56,128]{1,0:T(8,128)(2,1)} %bitcast.13, ...), custom_call_target="tpu_custom_call" | custom-call | tf_op jit(solution)/shard_map/pallas_call | solution.py:415
  73.1 3.7 %shard_map.180 = (bf16[64,7168]{1,0:T(8,128)(2,1)}, bf16[56,128]{1,0:T(8,128)(2,1)}, f32[7,64]{1,0:T(8,128)}, f32[7,64]{1,0:T(8,128)}, f32[7,64]{1,0:T(8,128)}, ...) custom-call(bf16[2,4,4,4,2,16,128]{6,5,4,3,2,1,0:T(8,128)(2,1)} %get-tuple-element.18.gathered_hbm, ...), custom_call_target="tpu_custom_call" | custom-call | tf_op jit(solution)/shard_map/pallas_call | solution.py:449

commit v3 on v2

--- a/solution.py
+++ b/solution.py
@@ -138,11 +138,11 @@
 def step_kernel(
     hidden_hbm, seg_hbm, key_hbm, weight_hbm, gain_hbm, table_hbm,
     wm_hbm, wf_hbm, ws_hbm, gm_hbm, gf_hbm, gs_hbm,
-    gathered_ref, adam_ref,
-    hidden_ref, seg_ref, key_ref, weight_ref, gain_ref, table_ref,
+    gathered_hbm, adam_ref,
+    gathered_ref, hidden_ref, seg_ref, key_ref, weight_ref, gain_ref, table_ref,
     wm_ref, wf_ref, ws_ref, gm_ref, gf_ref, gs_ref,
     squares, wide, segs, gains, packed_ref, shard_ref,
-    r1, sb, r2, zb, r3, hb, r4, shards, masters, in_sem, row_sem,
+    r1, sb, r2, zb, r3, hb, r4, mine, shards, masters, sums, in_sem, row_sem, met, out_sem,
     s1, t1, s2, t2, s3, t3, s4, t4, s5, t5, s6, t6, s7, t7, s8, t8,
 ):
     tokens, width = hidden_ref.shape
@@ -180,16 +180,22 @@
         load.start()
 
     sibling = device(core=1 - core)
-    plane = [(dx, dy) for dx in range(NX) for dy in range(NY)]
-    others = plane[1:]
+    order_x = sorted(range(NX), key=lambda d: (d == 0, -min(d, NX - d)))
+    order_y = sorted(range(NY), key=lambda d: -min(d, NY - d))
+    plane = [(dx, dy) for dx in order_x for dy in order_y]
+    others = [o for o in plane if o != (0, 0)]
     ahead = {o: (lax.rem(x + o[0], NX), lax.rem(y + o[1], NY)) for o in plane}
     behind = {o: (lax.rem(x + NX - o[0], NX), lax.rem(y + NY - o[1], NY)) for o in plane}
     up_near = [lax.rem(near + d, NEAR) for d in range(NEAR)]
+    quarters = [up_near[(t + 1) % NEAR] for t in range(NEAR)]
+    behind_near = [lax.rem(near + NEAR - d, NEAR) for d in range(NEAR)]
     up_far = [lax.rem(far + d, FAR) for d in range(FAR)]
     far_first = sorted(range(1, FAR), key=lambda d: -min(d, FAR - d))
 
     barrier = pltpu.get_barrier_semaphore()
-    peers = [device(far=up_far[d]) for d in far_first]
+    reach = [1 << i for i in range((FAR // 2).bit_length() - 1)]
+    steps = [[device(far=up_far[d]), device(far=up_far[FAR - d])] for d in reach]
+    peers = list(steps[0])
     peers += [device(near=n) for n in up_near[1:]]
     peers += [device(x=ahead[o][0], y=ahead[o][1]) for o in others]
     peers += [sibling]
@@ -227,82 +233,98 @@
         load.wait()
     gains[...] = gain_ref[...].astype(F32)
 
-    def block(k, carry):
-        columns = pl.ds(pl.multiple_of(k * BLOCK, LANES), BLOCK)
-        even, odd = gradient_block(
-            both, hidden_ref[:, columns], weight_ref[:, columns],
-            lambda i: gains[pl.ds(OWN * k + i, 1), :], wide,
-        )
-        n, h = lax.rem(k, NEAR), k // NEAR
-        for q in range(16):
-            xq, cq, yq = q // 4, (q // 2) % 2, 2 * (q % 2)
-            packed_ref[cq, xq, yq, n, h] = even[q]
-            packed_ref[cq, xq, yq + 1, n, h] = odd[q]
-        return carry
-
-    lax.fori_loop(0, width // BLOCK, block, 0)
+    pl.semaphore_wait(barrier, len(peers))
+    for peer in steps[0]:
+        pl.semaphore_signal(met.at[0], inc=1, device_id=peer, device_id_type=MESH)
+
+    def gradients(t):
+        n = quarters[t]
+        for h in range(SPAN):
+            k = h * NEAR + n
+            columns = pl.ds(pl.multiple_of(k * BLOCK, LANES), BLOCK)
+            even, odd = gradient_block(
+                both, hidden_ref[:, columns], weight_ref[:, columns],
+                lambda i: gains[pl.ds(OWN * k + i, 1), :], wide.at[h],
+            )
+            for q in range(16):
+                xq, cq, yq = q // 4, (q // 2) % 2, 2 * (q % 2)
+                packed_ref[t, cq, xq, yq, h] = even[q]
+                packed_ref[t, cq, xq, yq + 1, h] = odd[q]
+
+    def halves(t):
+        return send(packed_ref.at[t, 1 - core], r1.at[t], s1.at[t], t1.at[t], sibling)
+
+    def to_plane(t):
+        first[t].wait_recv()
+        sb[t] = (packed_ref[t, core].astype(F32) + r1[t].astype(F32)).astype(BF16)
+        for i, o in enumerate(others):
+            xs, ys = ahead[o]
+            send(sb.at[t, xs, ys], r2.at[t, i], s2, t2.at[t], device(x=xs, y=ys))
+
+    first = []
+    for t in range(NEAR):
+        gradients(t)
+        first.append(halves(t))
+        if t > 0:
+            to_plane(t - 1)
+        if t == NEAR - 1:
+            for i in range(1, len(steps)):
+                pl.semaphore_wait(met.at[i - 1], 2)
+                for peer in steps[i]:
+                    pl.semaphore_signal(met.at[i], inc=1, device_id=peer, device_id_type=MESH)
 
     for load in loads[5:]:
         load.wait()
     for a, states in enumerate(((wm_ref, gm_ref), (wf_ref, gf_ref), (ws_ref, gs_ref))):
         for p, row in enumerate(pack_shard(states)):
             shard_ref[4 * a + p : 4 * a + p + 1, :] = row
-    shard_ref[12:16, :] = jnp.ones((4, LANES), F32)
-
-    pl.semaphore_wait(barrier, len(peers))
-
-    first = [
-        send(packed_ref.at[1 - core, ahead[dx, 0][0]], r1.at[dx], s1.at[dx], t1.at[dx], sibling)
-        for dx in range(NX)
-    ]
-    swaps = [
-        send(shard_ref, shards.at[far], s8.at[d], t8.at[d], device(far=up_far[d]))
-        for d in far_first
-    ]
-    shards[far] = shard_ref[...]
-
-    second = []
-    for dx in range(NX):
-        xs = ahead[dx, 0][0]
-        first[dx].wait_recv()
-        sb[xs] = (packed_ref[core, xs].astype(F32) + r1[dx].astype(F32)).astype(BF16)
-        for dy in range(NY):
-            o = dx, dy
-            if o == (0, 0):
-                continue
-            ys = ahead[o][1]
-            slot = dx * NY + dy - 1
-            second.append(send(sb.at[xs, ys], r2.at[slot], s2.at[slot], t2.at[slot], device(x=xs, y=ys)))
-
-    total = sb[x, y].astype(F32)
-    for slot in range(len(others)):
-        second[slot].wait_recv()
-        total = total + r2[slot].astype(F32)
-    zb[...] = total.astype(BF16)
-
-    third = [
-        send(zb.at[up_near[d]], r3.at[d], s3.at[d], t3.at[d], device(near=up_near[d]))
-        for d in range(1, NEAR)
-    ]
+    shard = shard_ref[0:12, :]
+    master = shard[0:4].astype(BF16).astype(F32)
+    mine[...] = jnp.concatenate([master, shard[0:4] - master, shard[4:12]], axis=0).astype(BF16)
+
+    to_plane(NEAR - 1)
+
+    third = []
+    for t in range(NEAR):
+        pltpu.make_async_copy(r2.at[t], r2.at[t], t2.at[t]).wait()
+        total = sb[t, x, y].astype(F32)
+        for i in range(len(others)):
+            total = total + r2[t, i].astype(F32)
+        if t < NEAR - 1:
+            zb[t] = total.astype(BF16)
+            third.append(
+                send(zb.at[t], r3.at[t], s3.at[t], t3.at[t], device(near=quarters[t]))
+            )
+        if t == 0:
+            pl.semaphore_wait(met.at[len(steps) - 1], 2)
+            swaps = [
+                send(mine, shards.at[far], s8.at[d], t8.at[d], device(far=up_far[d]))
+                for d in far_first
+            ]
+            shards[far] = mine[...]
+    for t in range(NEAR - 1):
+        third[t].wait_recv()
+        total = total + r3[t].astype(F32)
+    hb[...] = total.astype(BF16)
+
+    fourth = [
+        send(hb, r4.at[far], s4.at[d], t4.at[d], device(far=up_far[d])) for d in far_first
+    ]
+    r4[far] = hb[...]
+    for c in first + third:
+        c.wait_send()
+    pltpu.make_async_copy(r2, r2, s2).wait()
 
     for c in swaps:
         c.wait_recv()
-    for a in range(3):
-        for f in range(FAR):
+    for f in range(FAR):
+        state = shards[f].astype(F32)
+        state = [state[0:4] + state[4:8], state[8:12], state[12:16]]
+        for a in range(3):
             for p in range(4):
                 row = p * NZH + f // SPAN
-                masters[a, f % SPAN, row : row + 1, :] = shards[f, 4 * a + p : 4 * a + p + 1, :]
-
-    total = zb[near].astype(F32)
-    for c, d in zip(third, range(1, NEAR)):
-        c.wait_recv()
-        total = total + r3[d].astype(F32)
-    hb[...] = total.astype(BF16)
-
-    fourth = [
-        send(hb, r4.at[far], s4.at[d], t4.at[d], device(far=up_far[d])) for d in far_first
-    ]
-    r4[far] = hb[...]
+                masters[a, f % SPAN, row : row + 1, :] = state[a][p : p + 1]
+
     for c in fourth:
         c.wait_recv()
     gradient = r4[0].astype(F32)
@@ -313,30 +335,54 @@
     is_gain = jnp.logical_and(iota(tile, 1) >= 3 * NZH, iota(tile, 2) >= ROPE)
     decay = jnp.where(is_gain, 0.0, 0.1)
     new = adamw(masters[0], masters[1], masters[2], gradient, decay)
-    for a in range(3):
-        adam_ref[a] = new[a]
-
-    own = gathered_ref.at[core, x, y]
-    gathered_ref[core, x, y, near] = new[0].astype(BF16)
+
+    own = gathered_ref.at[core, :, x, y]
+    gathered_ref[core, near, x, y] = new[0].astype(BF16)
     fifth = [
         send(own.at[near], own.at[near], s5.at[d], t5.at[d], device(near=up_near[d]))
         for d in range(1, NEAR)
     ]
+
+    sums[...] = gradient
+    zh = z // NZL
+    gradient = [sums[lax.rem(far, SPAN), pl.ds(p * NZH + zh, 1), :] for p in range(4)]
+    is_gain = jnp.logical_and(iota((4, LANES), 0) == 3, iota((4, LANES), 1) >= ROPE)
+    decay = jnp.where(is_gain, 0.0, 0.1)
+    shard = shard_ref[0:12, :]
+    new = adamw(shard[0:4], shard[4:8], shard[8:12], jnp.concatenate(gradient, axis=0), decay)
+    for a in range(3):
+        adam_ref[4 * a : 4 * a + 4, :] = new[a]
+    for c in swaps + fourth:
+        c.wait_send()
+
+    for d in range(NEAR):
+        if d > 0:
+            fifth[d - 1].wait_recv()
+        tile = own.at[behind_near[d]]
+        for o in others:
+            send(tile, tile, s6, t6.at[d], device(x=ahead[o][0], y=ahead[o][1]))
     for c in fifth:
-        c.wait_recv()
-    sixth = [
-        send(own, own, s6.at[i], t6.at[i], device(x=ahead[o][0], y=ahead[o][1]))
-        for i, o in enumerate(others)
-    ]
-    seventh = [send(own, own, s7.at[len(others)], t7.at[len(others)], sibling)]
-    for i, o in enumerate(others):
-        sixth[i].wait_recv()
-        part = gathered_ref.at[core, behind[o][0], behind[o][1]]
-        seventh.append(send(part, part, s7.at[i], t7.at[i], sibling))
-    for c in seventh:
-        c.wait_recv()
-    for c in first + swaps + second + third + fourth + fifth + sixth + seventh:
         c.wait_send()
+
+    out = []
+    for d in range(NEAR):
+        n = behind_near[d]
+        pltpu.make_async_copy(r2.at[d], r2.at[d], t6.at[d]).wait()
+        part = gathered_ref.at[core, n]
+        send(part, part, s7, t7.at[d], sibling)
+        out.append(pltpu.make_async_copy(part, gathered_hbm.at[core, n], out_sem.at[2 * d]))
+        out[-1].start()
+    for d in range(NEAR):
+        n = behind_near[d]
+        part = gathered_ref.at[1 - core, n]
+        pltpu.make_async_copy(part, part, t7.at[d]).wait()
+        out.append(pltpu.make_async_copy(part, gathered_hbm.at[1 - core, n], out_sem.at[2 * d + 1]))
+        out[-1].start()
+    pltpu.make_async_copy(r2, r2, s6).wait()
+    half = gathered_ref.at[0]
+    pltpu.make_async_copy(half, half, s7).wait()
+    for c in out:
+        c.wait()
 
 
 def unpack_kernel(
@@ -345,7 +391,7 @@
 ):
     loads = [
         pltpu.make_async_copy(
-            gathered_hbm.at[:, :, :, n], gathered_ref.at[:, :, :, n], in_sem.at[n]
+            gathered_hbm.at[:, n], gathered_ref.at[:, n], in_sem.at[n]
         )
         for n in range(NEAR)
     ]
@@ -362,8 +408,8 @@
         even, odd = [], []
         for q in range(16):
             x, core, y = q // 4, (q // 2) % 2, 2 * (q % 2)
-            even.append(gathered_ref[core, x, y, n, h].astype(F32).reshape(1, 16, LANES))
-            odd.append(gathered_ref[core, x, y + 1, n, h].astype(F32).reshape(1, 16, LANES))
+            even.append(gathered_ref[core, n, x, y, h].astype(F32).reshape(1, 16, LANES))
+            odd.append(gathered_ref[core, n, x, y + 1, h].astype(F32).reshape(1, 16, LANES))
         even, odd = jnp.concatenate(even, axis=0), jnp.concatenate(odd, axis=0)
         tiles = []
         for i in range(2):
@@ -384,11 +430,9 @@
             gains[at : at + 1, :] = jnp.sum(block[ROPE : ROPE + 8], axis=0, keepdims=True)
     gain_ref[...] = gains[...].astype(BF16)
     loads[NEAR].wait()
-    zh = lax.rem(lax.axis_index("inner"), NZH)
-    zl = lax.axis_index("outer") // (NC * NX)
     for a, (w, g) in enumerate(((wm_ref, gm_ref), (wf_ref, gf_ref), (ws_ref, gs_ref))):
         for p in range(4):
-            row = adam_ref[a, zl // NEAR, pl.ds(p * NZH + zh, 1), :]
+            row = adam_ref[4 * a + p : 4 * a + p + 1, :]
             w[2 * p : 2 * p + 1, :] = row[:, :ROPE]
             if p < 3:
                 w[2 * p + 1 : 2 * p + 2, :] = row[:, ROPE:]
@@ -411,33 +455,38 @@
     piece = (SPAN, 16, LANES)
     others = NX * NY - 1
     chunk = (NEAR, *piece)
-    counts = [NX, others, NEAR, FAR, NEAR, others, others + 1, FAR]
+    counts = [NEAR, NEAR, 0, NEAR, NEAR, NEAR, FAR, FAR, NEAR, NEAR, 0, NEAR, 0, NEAR, FAR, FAR]
     return pl.pallas_call(
         step_kernel,
-        out_shape=shapes(((NC, NX, NY, *chunk), BF16), ((3, *piece), F32)),
+        out_shape=shapes(((NC, NEAR, NX, NY, *piece), BF16), ((16, LANES), F32)),
         in_specs=[pl.BlockSpec(memory_space=pltpu.HBM)] * len(operands),
-        out_specs=[vmem()] * 2,
-        scratch_shapes=[pltpu.VMEM(o.shape, o.dtype) for o in operands]
+        out_specs=[pl.BlockSpec(memory_space=pltpu.HBM), vmem()],
+        scratch_shapes=[pltpu.VMEM((NC, NEAR, NX, NY, *piece), BF16)]
+        + [pltpu.VMEM(o.shape, o.dtype) for o in operands]
         + [
             pltpu.VMEM((2 * LANES, LANES), F32),
-            pltpu.VMEM((BLOCK, LANES), F32),
+            pltpu.VMEM((SPAN, BLOCK, LANES), F32),
             pltpu.VMEM((8, 2 * LANES), jnp.int32),
             pltpu.VMEM((width // LANES, LANES), F32),
-            pltpu.VMEM((NC, NX, NY, *chunk), BF16),
+            pltpu.VMEM((NEAR, NC, NX, NY, *piece), BF16),
             pltpu.VMEM((16, LANES), F32),
-            pltpu.VMEM((NX, NY, *chunk), BF16),
-            pltpu.VMEM((NX, NY, *chunk), BF16),
-            pltpu.VMEM((others, *chunk), BF16),
+            pltpu.VMEM((NEAR, NX, NY, *piece), BF16),
+            pltpu.VMEM((NEAR, NX, NY, *piece), BF16),
+            pltpu.VMEM((NEAR, others, *piece), BF16),
             pltpu.VMEM(chunk, BF16),
             pltpu.VMEM(chunk, BF16),
             pltpu.VMEM(piece, BF16),
             pltpu.VMEM((FAR, *piece), BF16),
-            pltpu.VMEM((FAR, 16, LANES), F32),
+            pltpu.VMEM((16, LANES), BF16),
+            pltpu.VMEM((FAR, 16, LANES), BF16),
             pltpu.VMEM((3, *piece), F32),
+            pltpu.VMEM(piece, F32),
             dma((len(operands) - 1,)),
             dma((tokens // ROWS,)),
+            pltpu.SemaphoreType.REGULAR((2,)),
+            dma((2 * NEAR,)),
         ]
-        + [dma((n,)) for n in counts for _ in range(2)],
+        + [dma((n,)) if n else dma for n in counts],
         compiler_params=pltpu.CompilerParams(
             collective_id=0, has_side_effects=True, vmem_limit_bytes=56 * 1024 * 1024
         ),

time: 77 us -> 68.2 us (0.89)
  Pallas kernels: 76.2 us -> 67.4 us
    pallas_call x1, Pallas kernels: 72.5 us -> 63.7 us  [step(): pl.pallas_call(step_kernel, out_shape=shapes(((NC, NEAR, NX, NY, *piece),...]
where the time goes in v3:
time: 68.2 us; the launch traced here: 68 us
  Pallas kernels  67.4 us (99%)
    pallas_call x1, Pallas kernels, step(): pl.pallas_call(step_kernel, out_shape=shapes(((NC, NEAR, NX, NY, *piece),...  63.7 us
    pallas_call x1, Pallas kernels, unpack(): pl.pallas_call(unpack_kernel, out_shape=shapes(((ROPE, width), BF16), ((w...  3.72 us

profile of v3, /device:TPU:1, one launch (start us, length us, event | category | flops | bytes accessed | tf_op | source)
XLA Modules:
  0.0 68.0 jit_solution(7558030551912238630)
XLA Ops:
  0.6 63.7 %shard_map.179 = (bf16[2,4,4,4,2,16,128]{6,5,4,3,2,1,0:T(8,128)(2,1)}, f32[16,128]{1,0:T(8,128)}) custom-call(bf16[240,7168]{1,0:T(8,128)(2,1)} %hidden_hbm.1, s32[1,240]{1,0:T(1,128)} %seg_hbm.1, bf16[64,240]{1,0:T(8,128)(2,1)} %bitcast.12, bf16[64,7168]{1,0:T(8,128)(2,1)} %bitcast.11, bf16[56,128]{1,0:T(8,128)(2,1)} %bitcast.13, ...), custom_call_target="tpu_custom_call" | custom-call | tf_op jit(solution)/shard_map/pallas_call | solution.py:459
  64.3 3.7 %shard_map.180 = (bf16[64,7168]{1,0:T(8,128)(2,1)}, bf16[56,128]{1,0:T(8,128)(2,1)}, f32[7,64]{1,0:T(8,128)}, f32[7,64]{1,0:T(8,128)}, f32[7,64]{1,0:T(8,128)}, ...) custom-call(bf16[2,4,4,4,2,16,128]{6,5,4,3,2,1,0:T(8,128)(2,1)} %get-tuple-element.18.gathered_hbm, ...), custom_call_target="tpu_custom_call" | custom-call | tf_op jit(solution)/shard_map/pallas_call | solution.py:498

commit v4 on v3

--- a/solution.py
+++ b/solution.py
@@ -1,3 +1,5 @@
+import functools
+
 import jax
 import jax.numpy as jnp
 import numpy as np
@@ -125,6 +127,35 @@
     return even, odd
 
 
+def unpack_block(tiles_ref, wide, weight_ref, gains_ref, k):
+    upper = iota((16, 8, LANES), 1) < 4
+    lane = iota((LANES, LANES), 1)
+    even, odd = [], []
+    for q in range(16):
+        x, core, y = q // 4, (q // 2) % 2, 2 * (q % 2)
+        even.append(tiles_ref[core, x, y].astype(F32).reshape(1, 16, LANES))
+        odd.append(tiles_ref[core, x, y + 1].astype(F32).reshape(1, 16, LANES))
+    even, odd = jnp.concatenate(even, axis=0), jnp.concatenate(odd, axis=0)
+    tiles = []
+    for i in range(2):
+        e, o = even[:, 8 * i : 8 * i + 8], odd[:, 8 * i : 8 * i + 8]
+        tiles.append(jnp.where(upper, e, pltpu.roll(o, 4, axis=1)))
+        tiles.append(jnp.where(upper, pltpu.roll(e, 4, axis=1), o))
+    tiles = [t.reshape(LANES, LANES) for t in tiles]
+    for r in range(OWN):
+        tile = tiles[r // 2]
+        if r % 2:
+            tile = pltpu.roll(tile, ROPE, axis=1)
+        gain = jnp.where(lane == ROPE + r, tiles[3], 0.0)
+        wide[pl.ds(r, LANES, stride=OWN), :] = jnp.where(lane < ROPE, tile, gain)
+    for i in range(OWN):
+        at = OWN * k + i
+        block = wide[i * LANES : (i + 1) * LANES, :].T
+        columns = pl.ds(pl.multiple_of(at * LANES, LANES), LANES)
+        weight_ref[:, columns] = block[:ROPE].astype(BF16)
+        gains_ref[pl.ds(at, 1), :] = jnp.sum(block[ROPE : ROPE + 8], axis=0, keepdims=True)
+
+
 def adamw(master, first, second, gradient, decay):
     first_new = beta_one * first + (1.0 - beta_one) * gradient
     second_new = beta_two * second + (1.0 - beta_two) * gradient * gradient
@@ -138,14 +169,15 @@
 def step_kernel(
     hidden_hbm, seg_hbm, key_hbm, weight_hbm, gain_hbm, table_hbm,
     wm_hbm, wf_hbm, ws_hbm, gm_hbm, gf_hbm, gs_hbm,
-    gathered_hbm, adam_ref,
-    gathered_ref, hidden_ref, seg_ref, key_ref, weight_ref, gain_ref, table_ref,
+    o0, o1, o2, o3, o4, o5, o6, o7,
+    gathered_ref, new_ref, low, hidden_ref, seg_ref, key_ref, weight_ref, gain_ref, table_ref,
     wm_ref, wf_ref, ws_ref, gm_ref, gf_ref, gs_ref,
     squares, wide, segs, gains, packed_ref, shard_ref,
     r1, sb, r2, zb, r3, hb, r4, mine, shards, masters, sums, in_sem, row_sem, met, out_sem,
     s1, t1, s2, t2, s3, t3, s4, t4, s5, t5, s6, t6, s7, t7, s8, t8,
 ):
     tokens, width = hidden_ref.shape
+    outs = (o0, o1, o2, o3, o4, o5, o6, o7)
     parts = tokens // ROWS
     outer, inner = lax.axis_index("outer"), lax.axis_index("inner")
     core, x = lax.rem(outer, NC), lax.rem(outer // NC, NX)
@@ -337,9 +369,9 @@
     new = adamw(masters[0], masters[1], masters[2], gradient, decay)
 
     own = gathered_ref.at[core, :, x, y]
-    gathered_ref[core, near, x, y] = new[0].astype(BF16)
+    gathered_ref[core, 0, x, y] = new[0].astype(BF16)
     fifth = [
-        send(own.at[near], own.at[near], s5.at[d], t5.at[d], device(near=up_near[d]))
+        send(own.at[0], own.at[d], s5.at[d], t5.at[d], device(near=up_near[d]))
         for d in range(1, NEAR)
     ]
 
@@ -350,34 +382,57 @@
     decay = jnp.where(is_gain, 0.0, 0.1)
     shard = shard_ref[0:12, :]
     new = adamw(shard[0:4], shard[4:8], shard[8:12], jnp.concatenate(gradient, axis=0), decay)
-    for a in range(3):
-        adam_ref[4 * a : 4 * a + 4, :] = new[a]
+    for a, (w, g) in enumerate(((wm_ref, gm_ref), (wf_ref, gf_ref), (ws_ref, gs_ref))):
+        for p in range(4):
+            row = new[a][p : p + 1]
+            w[2 * p : 2 * p + 1, :] = row[:, :ROPE]
+            if p < 3:
+                w[2 * p + 1 : 2 * p + 2, :] = row[:, ROPE:]
+            else:
+                g[...] = row[:, ROPE : ROPE + OWN]
+    out = [
+        pltpu.make_async_copy(src, dst, out_sem.at[i])
+        for i, (src, dst) in enumerate(
+            zip((wm_ref, wf_ref, ws_ref, gm_ref, gf_ref, gs_ref), outs[2:], strict=True)
+        )
+    ]
+    for c in out:
+        c.start()
     for c in swaps + fourth:
         c.wait_send()
 
     for d in range(NEAR):
         if d > 0:
             fifth[d - 1].wait_recv()
-        tile = own.at[behind_near[d]]
         for o in others:
-            send(tile, tile, s6, t6.at[d], device(x=ahead[o][0], y=ahead[o][1]))
+            send(own.at[d], own.at[d], s6, t6.at[d], device(x=ahead[o][0], y=ahead[o][1]))
     for c in fifth:
         c.wait_send()
 
-    out = []
+    def whole(d):
+        part = gathered_ref.at[1 - core, d]
+        pltpu.make_async_copy(part, part, t7.at[d]).wait()
+        for h in range(SPAN):
+            k = h * NEAR + behind_near[d]
+            unpack_block(gathered_ref.at[:, d, :, :, h], wide.at[h], new_ref, gains, k)
+            columns = pl.ds(pl.multiple_of(k * BLOCK, LANES), BLOCK)
+            out.append(
+                pltpu.make_async_copy(
+                    new_ref.at[:, columns], outs[0].at[:, columns], out_sem.at[len(out)]
+                )
+            )
+            out[-1].start()
+
     for d in range(NEAR):
-        n = behind_near[d]
         pltpu.make_async_copy(r2.at[d], r2.at[d], t6.at[d]).wait()
-        part = gathered_ref.at[core, n]
+        part = gathered_ref.at[core, d]
         send(part, part, s7, t7.at[d], sibling)
-        out.append(pltpu.make_async_copy(part, gathered_hbm.at[core, n], out_sem.at[2 * d]))
-        out[-1].start()
-    for d in range(NEAR):
-        n = behind_near[d]
-        part = gathered_ref.at[1 - core, n]
-        pltpu.make_async_copy(part, part, t7.at[d]).wait()
-        out.append(pltpu.make_async_copy(part, gathered_hbm.at[1 - core, n], out_sem.at[2 * d + 1]))
-        out[-1].start()
+        if d > 0:
+            whole(d - 1)
+    whole(NEAR - 1)
+    low[...] = gains[...].astype(BF16)
+    out.append(pltpu.make_async_copy(low, outs[1], out_sem.at[len(out)]))
+    out[-1].start()
     pltpu.make_async_copy(r2, r2, s6).wait()
     half = gathered_ref.at[0]
     pltpu.make_async_copy(half, half, s7).wait()
@@ -385,66 +440,25 @@
         c.wait()
 
 
-def unpack_kernel(
-    gathered_hbm, adam_hbm, weight_ref, gain_ref, wm_ref, wf_ref, ws_ref, gm_ref, gf_ref, gs_ref,
-    gathered_ref, adam_ref, wide, gains, in_sem,
-):
-    loads = [
-        pltpu.make_async_copy(
-            gathered_hbm.at[:, n], gathered_ref.at[:, n], in_sem.at[n]
-        )
-        for n in range(NEAR)
-    ]
-    loads.append(pltpu.make_async_copy(adam_hbm, adam_ref, in_sem.at[NEAR]))
-    for load in loads:
-        load.start()
-    upper = iota((16, 8, LANES), 1) < 4
-    lane = iota((LANES, LANES), 1)
-    for turn in range(NZL):
-        n, h = turn // SPAN, turn % SPAN
-        k = h * NEAR + n
-        if h == 0:
-            loads[n].wait()
-        even, odd = [], []
-        for q in range(16):
-            x, core, y = q // 4, (q // 2) % 2, 2 * (q % 2)
-            even.append(gathered_ref[core, n, x, y, h].astype(F32).reshape(1, 16, LANES))
-            odd.append(gathered_ref[core, n, x, y + 1, h].astype(F32).reshape(1, 16, LANES))
-        even, odd = jnp.concatenate(even, axis=0), jnp.concatenate(odd, axis=0)
-        tiles = []
-        for i in range(2):
-            e, o = even[:, 8 * i : 8 * i + 8], odd[:, 8 * i : 8 * i + 8]
-            tiles.append(jnp.where(upper, e, pltpu.roll(o, 4, axis=1)))
-            tiles.append(jnp.where(upper, pltpu.roll(e, 4, axis=1), o))
-        tiles = [t.reshape(LANES, LANES) for t in tiles]
-        for r in range(OWN):
-            tile = tiles[r // 2]
-            if r % 2:
-                tile = pltpu.roll(tile, ROPE, axis=1)
-            gain = jnp.where(lane == ROPE + r, tiles[3], 0.0)
-            wide[turn % 2, pl.ds(r, LANES, stride=OWN), :] = jnp.where(lane < ROPE, tile, gain)
-        for i in range(OWN):
-            at = OWN * k + i
-            block = wide[turn % 2, i * LANES : (i + 1) * LANES, :].T
-            weight_ref[:, at * LANES : (at + 1) * LANES] = block[:ROPE].astype(BF16)
-            gains[at : at + 1, :] = jnp.sum(block[ROPE : ROPE + 8], axis=0, keepdims=True)
-    gain_ref[...] = gains[...].astype(BF16)
-    loads[NEAR].wait()
-    for a, (w, g) in enumerate(((wm_ref, gm_ref), (wf_ref, gf_ref), (ws_ref, gs_ref))):
-        for p in range(4):
-            row = adam_ref[4 * a + p : 4 * a + p + 1, :]
-            w[2 * p : 2 * p + 1, :] = row[:, :ROPE]
-            if p < 3:
-                w[2 * p + 1 : 2 * p + 2, :] = row[:, ROPE:]
-            else:
-                g[...] = row[:, ROPE : ROPE + OWN]
-
-
-def vmem():
-    return pl.BlockSpec(memory_space=pltpu.VMEM)
-
-
-def shapes(*items):
+def copy_kernel(n, *refs):
+    src, dst, by, (sem_in, sem_out) = refs[:n], refs[n : 2 * n], refs[2 * n : 3 * n], refs[3 * n :]
+    rows = [pl.ds(16 * i, 16) for i in range(src[0].shape[0] // 16)]
+    ways = [tuple(ref[0].at[r] for ref in (src, by, dst)) for r in rows]
+    ways += list(zip(src[1:], by[1:], dst[1:], strict=True))
+    copies_in = [pltpu.make_async_copy(a, b, sem_in.at[i]) for i, (a, b, _) in enumerate(ways)]
+    copies_out = [pltpu.make_async_copy(b, c, sem_out.at[i]) for i, (_, b, c) in enumerate(ways)]
+    for c in copies_in:
+        c.start()
+    for c, after in zip(copies_in, copies_out, strict=True):
+        c.wait()
+        after.start()
+    for c in copies_out:
+        c.wait()
+
+
+def results(width):
+    items = [((ROPE, width), BF16), ((width // LANES, LANES), BF16)]
+    items += [((OWN, ROPE), F32)] * 3 + [((1, OWN), F32)] * 3
     return [jax.ShapeDtypeStruct(s, t) for s, t in items]
 
 
@@ -458,10 +472,14 @@
     counts = [NEAR, NEAR, 0, NEAR, NEAR, NEAR, FAR, FAR, NEAR, NEAR, 0, NEAR, 0, NEAR, FAR, FAR]
     return pl.pallas_call(
         step_kernel,
-        out_shape=shapes(((NC, NEAR, NX, NY, *piece), BF16), ((16, LANES), F32)),
+        out_shape=results(width),
         in_specs=[pl.BlockSpec(memory_space=pltpu.HBM)] * len(operands),
-        out_specs=[pl.BlockSpec(memory_space=pltpu.HBM), vmem()],
-        scratch_shapes=[pltpu.VMEM((NC, NEAR, NX, NY, *piece), BF16)]
+        out_specs=[pl.BlockSpec(memory_space=pltpu.HBM)] * 8,
+        scratch_shapes=[
+            pltpu.VMEM((NC, NEAR, NX, NY, *piece), BF16),
+            pltpu.VMEM((ROPE, width), BF16),
+            pltpu.VMEM((width // LANES, LANES), BF16),
+        ]
         + [pltpu.VMEM(o.shape, o.dtype) for o in operands]
         + [
             pltpu.VMEM((2 * LANES, LANES), F32),
@@ -484,7 +502,7 @@
             dma((len(operands) - 1,)),
             dma((tokens // ROWS,)),
             pltpu.SemaphoreType.REGULAR((2,)),
-            dma((2 * NEAR,)),
+            dma((6 + NZL + 1,)),
         ]
         + [dma((n,)) if n else dma for n in counts],
         compiler_params=pltpu.CompilerParams(
@@ -493,22 +511,18 @@
     )(*operands)
 
 
-def unpack(gathered, adam, width):
-    own = [((OWN, ROPE), F32)] * 3 + [((1, OWN), F32)] * 3
+def hand_on(arrays):
+    hbm = [pl.BlockSpec(memory_space=pltpu.HBM)] * len(arrays)
+    copies = arrays[0].shape[0] // 16 + len(arrays) - 1
     return pl.pallas_call(
-        unpack_kernel,
-        out_shape=shapes(((ROPE, width), BF16), ((width // LANES, LANES), BF16), *own),
-        in_specs=[pl.BlockSpec(memory_space=pltpu.HBM)] * 2,
-        out_specs=[vmem()] * 8,
-        scratch_shapes=[
-            pltpu.VMEM(gathered.shape, gathered.dtype),
-            pltpu.VMEM(adam.shape, adam.dtype),
-            pltpu.VMEM((2, BLOCK, LANES), F32),
-            pltpu.VMEM((width // LANES, LANES), F32),
-            pltpu.SemaphoreType.DMA((NEAR + 1,)),
-        ],
+        functools.partial(copy_kernel, len(arrays)),
+        out_shape=[jax.ShapeDtypeStruct(a.shape, a.dtype) for a in arrays],
+        in_specs=hbm,
+        out_specs=hbm,
+        scratch_shapes=[pltpu.VMEM(a.shape, a.dtype) for a in arrays]
+        + [pltpu.SemaphoreType.DMA((copies,))] * 2,
         compiler_params=pltpu.CompilerParams(vmem_limit_bytes=56 * 1024 * 1024),
-    )(gathered, adam)
+    )(*arrays)
 
 
 def shards(
@@ -519,8 +533,8 @@
     states = [weight_master, weight_first, weight_second]
     states += [g.reshape(1, OWN) for g in (gain_master, gain_first, gain_second)]
     operands = [hidden, segment_ids, key_grad.T, weight_bf16.T, gain_bf16.reshape(width // LANES, LANES)]
-    gathered, adam = step([*operands, jnp.asarray(rotary_table()), *states])
-    weight_t, gain, wm, wf, ws, gm, gf, gs = unpack(gathered, adam, width)
+    arrays = step([*operands, jnp.asarray(rotary_table()), *states])
+    weight_t, gain, wm, wf, ws, gm, gf, gs = hand_on(arrays)
     return (
         wm, wf, ws, gm.reshape(OWN), gf.reshape(OWN), gs.reshape(OWN), weight_t.T, gain.reshape(width)
     )

time: 68.2 us -> 66.8 us (0.979)
  Pallas kernels: 67.4 us -> 66 us
    pallas_call x2, Pallas kernels: 67.4 us -> 66 us  [the longest x1 63.8 us: step(): pl.pallas_call(step_kernel, out_shape=results(width), in_specs=[pl.BlockS...]
where the time goes in v4:
time: 66.8 us; the launch traced here: 66.6 us
  Pallas kernels  66 us (99%)
    pallas_call x1, Pallas kernels, step(): pl.pallas_call(step_kernel, out_shape=results(width), in_specs=[pl.BlockS...  63.8 us
    pallas_call x1, Pallas kernels, hand_on(): pl.pallas_call(functools.partial(copy_kernel, len(arrays)), out_shape=[ja...  2.18 us

profile of v4, /device:TPU:1, one launch (start us, length us, event | category | flops | bytes accessed | tf_op | source)
XLA Modules:
  0.0 66.6 jit_solution(12084261578988899161)
XLA Ops:
  0.6 63.8 %shard_map.179 = (bf16[64,7168]{1,0:T(8,128)(2,1)}, bf16[56,128]{1,0:T(8,128)(2,1)}, f32[7,64]{1,0:T(8,128)}, f32[7,64]{1,0:T(8,128)}, f32[7,64]{1,0:T(8,128)}, ...) custom-call(bf16[240,7168]{1,0:T(8,128)(2,1)} %hidden_hbm.1, s32[1,240]{1,0:T(1,128)} %seg_hbm.1, ...), custom_call_target="tpu_custom_call" | custom-call | tf_op jit(solution)/shard_map/pallas_call | solution.py:473
  64.4 2.2 %shard_map.180 = (bf16[64,7168]{1,0:T(8,128)(2,1)}, bf16[56,128]{1,0:T(8,128)(2,1)}, f32[7,64]{1,0:T(8,128)}, f32[7,64]{1,0:T(8,128)}, f32[7,64]{1,0:T(8,128)}, ...) custom-call(bf16[64,7168]{1,0:T(8,128)(2,1)} %get-tuple-element.24.refs_0_, ...), custom_call_target="tpu_custom_call" | custom-call | tf_op jit(solution)/shard_map/pallas_call | solution.py:517

commit v5 on v4

--- a/solution.py
+++ b/solution.py
@@ -375,6 +375,12 @@
         for d in range(1, NEAR)
     ]
 
+    def to_all(d):
+        for o in others:
+            send(own.at[d], own.at[d], s6, t6.at[d], device(x=ahead[o][0], y=ahead[o][1]))
+
+    to_all(0)
+
     sums[...] = gradient
     zh = z // NZL
     gradient = [sums[lax.rem(far, SPAN), pl.ds(p * NZH + zh, 1), :] for p in range(4)]
@@ -398,16 +404,10 @@
     ]
     for c in out:
         c.start()
-    for c in swaps + fourth:
-        c.wait_send()
-
-    for d in range(NEAR):
-        if d > 0:
-            fifth[d - 1].wait_recv()
-        for o in others:
-            send(own.at[d], own.at[d], s6, t6.at[d], device(x=ahead[o][0], y=ahead[o][1]))
-    for c in fifth:
-        c.wait_send()
+
+    for d in range(1, NEAR):
+        fifth[d - 1].wait_recv()
+        to_all(d)
 
     def whole(d):
         part = gathered_ref.at[1 - core, d]
@@ -433,6 +433,8 @@
     low[...] = gains[...].astype(BF16)
     out.append(pltpu.make_async_copy(low, outs[1], out_sem.at[len(out)]))
     out[-1].start()
+    for c in swaps + fourth + fifth:
+        c.wait_send()
     pltpu.make_async_copy(r2, r2, s6).wait()
     half = gathered_ref.at[0]
     pltpu.make_async_copy(half, half, s7).wait()

time: 66.8 us -> 66.8 us (level)
  no operation moved by 1% of the time
where the time goes in v5:
time: 66.8 us; the launch traced here: 66.6 us
  Pallas kernels  66 us (99%)
    pallas_call x1, Pallas kernels, step(): pl.pallas_call(step_kernel, out_shape=results(width), in_specs=[pl.BlockS...  63.8 us
    pallas_call x1, Pallas kernels, hand_on(): pl.pallas_call(functools.partial(copy_kernel, len(arrays)), out_shape=[ja...  2.18 us

profile of v5, /device:TPU:1, one launch (start us, length us, event | category | flops | bytes accessed | tf_op | source)
XLA Modules:
  0.0 66.6 jit_solution(7121646674190583130)
XLA Ops:
  0.6 63.8 %shard_map.179 = (bf16[64,7168]{1,0:T(8,128)(2,1)}, bf16[56,128]{1,0:T(8,128)(2,1)}, f32[7,64]{1,0:T(8,128)}, f32[7,64]{1,0:T(8,128)}, f32[7,64]{1,0:T(8,128)}, ...) custom-call(bf16[240,7168]{1,0:T(8,128)(2,1)} %hidden_hbm.1, s32[1,240]{1,0:T(1,128)} %seg_hbm.1, ...), custom_call_target="tpu_custom_call" | custom-call | tf_op jit(solution)/shard_map/pallas_call | solution.py:475
  64.4 2.2 %shard_map.180 = (bf16[64,7168]{1,0:T(8,128)(2,1)}, bf16[56,128]{1,0:T(8,128)(2,1)}, f32[7,64]{1,0:T(8,128)}, f32[7,64]{1,0:T(8,128)}, f32[7,64]{1,0:T(8,128)}, ...) custom-call(bf16[64,7168]{1,0:T(8,128)(2,1)} %get-tuple-element.24.refs_0_, ...), custom_call_target="tpu_custom_call" | custom-call | tf_op jit(solution)/shard_map/pallas_call | solution.py:519
